TPU v7x, 256 devices: a whole 4x4x8 slice. The times are simulated.
256 devices in a mesh: wide: 32 (over z, x_lo, core), narrow: 8 (over x_hi, y).
Axes of the slice: x: 4 (x_hi: 2, x_lo: 2; x = x_hi * 2 + x_lo), y: 4, z: 8, core: 2. Of those that a mesh axis runs over, the one named last changes fastest.
Arguments:
- inputs: bfloat16 [768, 6144], P('wide', 'narrow'), may hold values from -60 to 60, as said below
- cotangent: bfloat16 [768, 6144], P('wide', 'narrow'), may hold values from -6 to 6
- norm_gain: float32 [6144], P('narrow'), may hold values from 0.25 to 1.75
- q_gain: float32 [128], replicated, may hold values from 0.5 to 2
- k_gain: float32 [128], replicated, may hold values from 0.5 to 2
- w_query: bfloat16 [6144, 4096], P('narrow', 'wide'), may hold values from -0.078125 to 0.078125
- w_key: bfloat16 [6144, 4096], P('narrow', 'wide'), may hold values from -0.078125 to 0.078125
- w_value: bfloat16 [6144, 4096], P('narrow', 'wide'), may hold values from -0.078125 to 0.078125
- w_out: bfloat16 [4096, 6144], P('wide', 'narrow'), may hold values from -0.09375 to 0.09375
- w_up: bfloat16 [6144, 24576], P('narrow', 'wide'), may hold values from -0.078125 to 0.078125
- w_down: bfloat16 [24576, 6144], P('wide', 'narrow'), may hold values from -0.0390625 to 0.0390625
Outputs:
- d_inputs: bfloat16 [768, 6144], P('wide', 'narrow')
- grad_query: bfloat16 [6144, 4096], P('narrow', 'wide')
- grad_key: bfloat16 [6144, 4096], P('narrow', 'wide')
- grad_value: bfloat16 [6144, 4096], P('narrow', 'wide')
- grad_out: bfloat16 [4096, 6144], P('wide', 'narrow')
- grad_up: bfloat16 [6144, 24576], P('narrow', 'wide')
- grad_down: bfloat16 [24576, 6144], P('wide', 'narrow')
- grad_norm_gain: float32 [6144], P('narrow')
- grad_qgain: float32 [128], replicated
- grad_kgain: float32 [128], replicated
Inputs may be any that keep to these rules, and one draw needn't show every extreme that they name: `inputs`: activations entering the layer.
All inputs are finite; a program needn't handle non-finite values.
Results may differ from a plain program's by a relative error of at most 0.024.
Values may be sent and summed in bfloat16 or wider, within the bound.
A program may use at most 64 MiB of HBM per device.

v0:
```python
import jax
import jax.numpy as jnp
from jax import lax
from jax.sharding import PartitionSpec as P

PATCHES = 256


epsilon = 1e-06


def head_norm(matrix):
    centre = jnp.mean(matrix, axis=-1, keepdims=True)
    shifted = matrix - centre
    inv_std = lax.rsqrt(jnp.mean(shifted * shifted, axis=-1, keepdims=True) + epsilon)
    return (shifted * inv_std, inv_std)


def norm_back(upstream, normal, inv_std):
    first = jnp.mean(upstream, axis=-1, keepdims=True)
    second = jnp.mean(upstream * normal, axis=-1, keepdims=True)
    return inv_std * (upstream - first - normal * second)


def gelu_tanh(matrix):
    return jax.nn.gelu(matrix, approximate=True)


def product(left, right):
    return jnp.dot(left, right, preferred_element_type=jnp.float32)


def contract_last(left, right):
    return lax.dot_general(
        left, right, (((1,), (1,)), ((), ())), preferred_element_type=jnp.float32
    )


def contract_first(left, right):
    return lax.dot_general(
        left, right, (((0,), (0,)), ((), ())), preferred_element_type=jnp.float32
    )


def per_device(
    inputs, cotangent, norm_gain, q_gain, k_gain, w_query, w_key, w_value, w_out, w_up, w_down
):
    tok_rows = inputs.shape[0]
    full_width = inputs.shape[1] * lax.axis_size("narrow")
    all_tokens = tok_rows * lax.axis_size("wide")
    images = all_tokens // PATCHES
    head_dim = q_gain.shape[0]
    heads_here = w_query.shape[1] // head_dim
    as_float = inputs.astype(jnp.float32)
    totals = lax.psum((jnp.sum(as_float, axis=1), jnp.sum(as_float * as_float, axis=1)), "narrow")
    row_mean = (totals[0] / full_width)[:, None]
    row_var = totals[1][:, None] / full_width - row_mean * row_mean
    row_rstd = lax.rsqrt(row_var + epsilon)
    unit_rows = (as_float - row_mean) * row_rstd
    own_normed = (unit_rows * norm_gain).astype(jnp.bfloat16)
    normed = lax.all_gather(own_normed, "wide", axis=0, tiled=True)
    grad_rows = lax.all_gather(cotangent, "wide", axis=0, tiled=True)
    query, key_proj, value_sum, up_proj = lax.psum(
        (
            product(normed, w_query),
            product(normed, w_key),
            product(normed, w_value),
            product(normed, w_up),
        ),
        "narrow",
    )

    def split_heads(matrix):
        return matrix.reshape(images, PATCHES, heads_here, head_dim)

    q_unit, q_rstd = head_norm(split_heads(query))
    k_unit, k_rstd = head_norm(split_heads(key_proj))
    values = split_heads(value_sum.astype(jnp.bfloat16))
    q_normed = (q_unit * q_gain).astype(jnp.bfloat16)
    k_normed = (k_unit * k_gain).astype(jnp.bfloat16)
    score_scale = head_dim ** (-0.5)
    scores = (
        jnp.einsum("iphd,iqhd->ihpq", q_normed, k_normed, preferred_element_type=jnp.float32)
        * score_scale
    )
    exponent = jnp.exp(scores)
    softmax_probs = exponent / jnp.sum(exponent, axis=-1, keepdims=True)
    prob_low = softmax_probs.astype(jnp.bfloat16)
    attended = jnp.einsum("ihpq,iqhd->iphd", prob_low, values, preferred_element_type=jnp.float32)
    attended = attended.reshape(all_tokens, heads_here * head_dim).astype(jnp.bfloat16)
    gelu_out, gelu_pull = jax.vjp(gelu_tanh, up_proj)
    hidden = gelu_out.astype(jnp.bfloat16)
    d_att_sum, d_hidden = lax.psum(
        (contract_last(grad_rows, w_out), contract_last(grad_rows, w_down)), "narrow"
    )
    d_att = d_att_sum.astype(jnp.bfloat16)
    grad_out = contract_first(attended, grad_rows).astype(jnp.bfloat16)
    grad_down = contract_first(hidden, grad_rows).astype(jnp.bfloat16)
    d_up = gelu_pull(d_hidden)[0].astype(jnp.bfloat16)
    d_heads = split_heads(d_att)
    d_probs = jnp.einsum("iphd,iqhd->ihpq", d_heads, values, preferred_element_type=jnp.float32)
    d_values = jnp.einsum("ihpq,iphd->iqhd", prob_low, d_heads, preferred_element_type=jnp.float32)
    d_values = d_values.reshape(all_tokens, heads_here * head_dim).astype(jnp.bfloat16)
    d_scores = (
        softmax_probs * (d_probs - jnp.sum(softmax_probs * d_probs, axis=-1, keepdims=True))
    ).astype(jnp.bfloat16)
    d_qnorm = (
        jnp.einsum("ihpq,iqhd->iphd", d_scores, k_normed, preferred_element_type=jnp.float32)
        * score_scale
    )
    d_knorm = (
        jnp.einsum("ihpq,iphd->iqhd", d_scores, q_normed, preferred_element_type=jnp.float32)
        * score_scale
    )
    qgain_part = jnp.sum(d_qnorm * q_unit, axis=(0, 1, 2))
    kgain_part = jnp.sum(d_knorm * k_unit, axis=(0, 1, 2))
    d_query = (
        norm_back(d_qnorm * q_gain, q_unit, q_rstd)
        .reshape(all_tokens, heads_here * head_dim)
        .astype(jnp.bfloat16)
    )
    d_key = (
        norm_back(d_knorm * k_gain, k_unit, k_rstd)
        .reshape(all_tokens, heads_here * head_dim)
        .astype(jnp.bfloat16)
    )
    grad_query = contract_first(normed, d_query).astype(jnp.bfloat16)
    grad_key = contract_first(normed, d_key).astype(jnp.bfloat16)
    grad_value = contract_first(normed, d_values).astype(jnp.bfloat16)
    grad_up = contract_first(normed, d_up).astype(jnp.bfloat16)
    attention_share = lax.psum_scatter(
        (
            contract_last(d_query, w_query)
            + contract_last(d_key, w_key)
            + contract_last(d_values, w_value)
        ).astype(jnp.bfloat16),
        "wide",
        scatter_dimension=0,
        tiled=True,
    ).astype(jnp.float32)
    mlp_share = lax.psum_scatter(
        contract_last(d_up, w_up).astype(jnp.bfloat16), "wide", scatter_dimension=0, tiled=True
    ).astype(jnp.float32)
    d_normed = attention_share + mlp_share
    d_unit = d_normed * norm_gain
    grad_totals = lax.psum((jnp.sum(d_unit, axis=1), jnp.sum(d_unit * unit_rows, axis=1)), "narrow")
    first = (grad_totals[0] / full_width)[:, None]
    second = (grad_totals[1] / full_width)[:, None]
    d_inputs = (
        cotangent.astype(jnp.float32) + row_rstd * (d_unit - first - unit_rows * second)
    ).astype(jnp.bfloat16)
    gain_part = jnp.sum(d_normed * unit_rows, axis=0)
    grad_norm_gain, grad_qgain, grad_kgain = lax.psum((gain_part, qgain_part, kgain_part), "wide")
    return (
        d_inputs,
        grad_query,
        grad_key,
        grad_value,
        grad_out,
        grad_up,
        grad_down,
        grad_norm_gain,
        grad_qgain,
        grad_kgain,
    )


def solution(mesh):
    return jax.shard_map(
        per_device,
        mesh=mesh,
        in_specs=(
            P("wide", "narrow"),
            P("wide", "narrow"),
            P("narrow"),
            P(),
            P(),
            P("narrow", "wide"),
            P("narrow", "wide"),
            P("narrow", "wide"),
            P("wide", "narrow"),
            P("narrow", "wide"),
            P("wide", "narrow"),
        ),
        out_specs=(
            P("wide", "narrow"),
            P("narrow", "wide"),
            P("narrow", "wide"),
            P("narrow", "wide"),
            P("wide", "narrow"),
            P("narrow", "wide"),
            P("wide", "narrow"),
            P("narrow"),
            P(),
            P(),
        ),
        check_vma=False,
    )
```

profile of v0, /device:TPU:1, one launch (start us, length us, event | category | flops | bytes accessed | tf_op | source)
XLA Modules:
  0.0 649.6 jit_solution(5543110064634051939)
XLA Ops:
  8.3 21.5 %all-reduce.3 = (f32[24]{0:T(128)S(1)}, f32[24]{0:T(128)S(1)}) all-reduce(f32[24]{0:T(128)S(1)} %get-tuple-element.20, f32[24]{0:T(128)S(1)} %get-tuple-element.19), channel_id=1, replica_groups=mesh['wide'=32,'narrow'=8] {'narrow'}, use_global_device_ids=true, to_apply=%region_3.0 | all-reduce | flops 48 | bytes 384 | tf_op jit(solution)/shard_map/psum | solution.py:55
  32.6 66.0 %all-gather.3.cloned.1.call-done = bf16[768,768]{1,0:T(8,128)(2,1)} async-done(((bf16[24,768]{1,0:T(8,128)(2,1)}), bf16[768,768]{1,0:T(8,128)(2,1)}) %all-gather.3.cloned.1.call-update) | async-done | bytes 1179664 | tf_op jit(solution)/shard_map/all_gather | solution.py:61
  98.6 2.6 fusion.50
  102.4 2.5 fusion.57
  104.9 59.1 %all-gather.5.cloned.1.call-done = bf16[768,768]{1,0:T(8,128)(2,1)} async-done(((bf16[24,768]{1,0:T(8,128)(2,1)}), bf16[768,768]{1,0:T(8,128)(2,1)}) %all-gather.5.cloned.1.call-update) | async-done | bytes 1179664 | tf_op jit(solution)/shard_map/all_gather | solution.py:62
  164.1 3.8 fusion.56
  169.6 2.1 fusion.51
  172.7 56.2 %all-reduce.9 = (bf16[768,128]{1,0:T(8,128)(2,1)S(1)}, bf16[768,128]{1,0:T(8,128)(2,1)S(1)}) all-reduce(f32[768,128]{1,0:T(8,128)S(1)} %copy-done.13, f32[768,128]{1,0:T(8,128)S(1)} %fusion.52), channel_id=1, replica_groups=mesh['wide'=32,'narrow'=8] {'narrow'}, use_global_device_ids=true, to_apply=%region_11.0 | all-reduce | flops 196608 | bytes 1179648 | tf_op jit(solution)/shard_map/psum | solution.py:93
  230.1 88.4 %all-reduce.8.cloned.1.call-done = (f32[768,768]{1,0:T(8,128)}, f32[768,768]{1,0:T(8,128)}, f32[768,128]{1,0:T(8,128)}, f32[768,128]{1,0:T(8,128)}) async-done(((f32[768,768]{1,0:T(8,128)}, f32[768,768]{1,0:T(8,128)}, f32[768,128]{1,0:T(8,128)}, f32[768,128]{1,0:T(8,128)}), (f32[768,768]{1,0:T(8,128)}, f32[768,768]{1,0:T(8,128)}, f32[768,128]{1,0:T(8,128)}, ...) | async-done | bytes 5505040 | tf_op jit(solution)/shard_map/psum | solution.py:63
  320.9 1.6 multiply_reduce_fusion.1
  322.5 3.9 fusion.6
  327.5 2.1 convolution_convert_fusion.2
  333.4 2.5 multiply_reduce_fusion
  339.8 1.7 copy.39
  342.4 2.2 fusion.14
  345.5 1.8 copy.42
  353.3 1.9 fusion.13
  361.2 2.1 convolution_convert_fusion.1
  363.4 2.4 convolution_convert_fusion
  365.7 74.7 %reduce-scatter.5.cloned.1.call-done = bf16[24,768]{1,0:T(8,128)(2,1)} async-done(((bf16[768,768]{1,0:T(8,128)(2,1)}), bf16[24,768]{1,0:T(8,128)(2,1)}) %reduce-scatter.5.cloned.1.call-update) | async-done | bytes 36880 | tf_op jit(solution)/shard_map/reduce_scatter | solution.py:141
  440.5 117.6 %reduce-scatter.3.cloned.1.call-done = bf16[24,768]{1,0:T(8,128)(2,1)} async-done(((bf16[768,768]{1,0:T(8,128)(2,1)}), bf16[24,768]{1,0:T(8,128)(2,1)}) %reduce-scatter.3.cloned.1.call-update) | async-done | bytes 36880 | tf_op jit(solution)/shard_map/reduce_scatter | solution.py:131
  559.1 20.5 %all-reduce.1 = (f32[24]{0:T(128)S(1)}, f32[24]{0:T(128)S(1)}) all-reduce(f32[24]{0:T(128)S(1)} %get-tuple-element.17, f32[24]{0:T(128)S(1)} %get-tuple-element.18), channel_id=1, replica_groups=mesh['wide'=32,'narrow'=8] {'narrow'}, use_global_device_ids=true, to_apply=%region_25.0 | all-reduce | flops 48 | bytes 384 | tf_op jit(solution)/shard_map/psum | solution.py:146
  579.6 62.0 %all-reduce = (f32[768]{0:T(1024)}, f32[128]{0:T(128)}, f32[128]{0:T(128)}) all-reduce(f32[768]{0:T(1024)S(1)} %get-tuple-element.16, f32[128]{0:T(128)S(1)} %copy-done.33, f32[128]{0:T(128)S(1)} %copy-done.34), channel_id=1, replica_groups=mesh['wide'=32,'narrow'=8] {'wide'}, use_global_device_ids=true, to_apply=%region_27.0 | all-reduce | flops 1024 | bytes 8192 | tf_op jit(solution)/shard_map/psum | solution.py:153
  641.6 1.5 fusion.39
  (131 shorter events, 34.6 us)
Async XLA Ops:
  7.2 95.2 %copy-start = (bf16[768,768]{1,0:T(8,128)(2,1)S(1)}, bf16[768,768]{1,0:T(8,128)(2,1)}, u32[]{:S(2)}) copy-start(bf16[768,768]{1,0:T(8,128)(2,1)} %param.20) | copy-start | bytes 3538948
  7.2 94.0 %copy-start.22 = (bf16[768,128]{1,0:T(8,128)(2,1)S(1)}, bf16[768,128]{1,0:T(8,128)(2,1)}, u32[]{:S(2)}) copy-start(bf16[768,128]{1,0:T(8,128)(2,1)} %param.16) | copy-start | bytes 589828
  7.2 91.4 %all-gather.3.cloned.1.call-start = ((), (), s32[]{:S(2)}) async-start(), calls=%async_computation.2 | async-start | bytes 1216512 | tf_op jit(solution)/shard_map/all_gather | solution.py:61
  31.8 132.3 %all-gather.5.cloned.1.call-start = ((), (), s32[]{:S(2)}) async-start(), calls=%async_computation.3 | async-start | bytes 1216512 | tf_op jit(solution)/shard_map/all_gather | solution.py:62
  32.6 285.9 %all-reduce.8.cloned.1.call-start = ((), (), s32[]{:S(2)}) async-start(), calls=%async_computation.6 | async-start | bytes 11010048 | tf_op jit(solution)/shard_map/psum | solution.py:63
  98.6 2.6 copy-start.1
  102.4 61.7 %copy-start.38 = (bf16[768,768]{1,0:T(8,128)(2,1)S(1)}, bf16[768,768]{1,0:T(8,128)(2,1)}, u32[]{:S(2)}) copy-start(bf16[768,768]{1,0:T(8,128)(2,1)} %param.21) | copy-start | bytes 3538948
  167.9 272.5 %reduce-scatter.5.cloned.1.call-start = ((), (), s32[]{:S(2)}) async-start(), calls=%async_computation.5 | async-start | bytes 1216512 | tf_op jit(solution)/shard_map/reduce_scatter | solution.py:141
  168.6 3.2 copy-start.17
  228.9 93.6 %copy-start.19 = (bf16[768,128]{1,0:T(8,128)(2,1)}, bf16[768,128]{1,0:T(8,128)(2,1)S(1)}, u32[]{:S(2)}) copy-start(bf16[768,128]{1,0:T(8,128)(2,1)S(1)} %get-tuple-element.27) | copy-start | bytes 589828
  228.9 93.6 %copy-start.20 = (bf16[768,128]{1,0:T(8,128)(2,1)}, bf16[768,128]{1,0:T(8,128)(2,1)S(1)}, u32[]{:S(2)}) copy-start(bf16[768,128]{1,0:T(8,128)(2,1)S(1)} %get-tuple-element.26) | copy-start | bytes 589828
  329.6 228.4 %reduce-scatter.3.cloned.1.call-start = ((), (), s32[]{:S(2)}) async-start(), calls=%async_computation.4 | async-start | bytes 1216512 | tf_op jit(solution)/shard_map/reduce_scatter | solution.py:131
  342.4 2.3 copy-start.7
  342.4 2.3 copy-start.31
  342.4 4.8 copy-start.21
  345.5 3.9 copy-start.10
  355.1 2.3 copy-start.12
  363.3 194.8 %copy-start.24 = (bf16[24,768]{1,0:T(8,128)(2,1)S(1)}, bf16[24,768]{1,0:T(8,128)(2,1)}, u32[]{:S(2)}) copy-start(bf16[24,768]{1,0:T(8,128)(2,1)} %param.11) | copy-start | bytes 110596
  363.3 194.8 %copy-start.26 = (f32[768]{0:T(1024)S(1)}, f32[768]{0:T(1024)}, u32[]{:S(2)}) copy-start(f32[768]{0:T(1024)} %param.13) | copy-start | bytes 9220
  363.3 194.8 %copy-start.28 = (f32[24]{0:T(128)S(1)}, f32[24]{0:T(128)}, u32[]{:S(2)}) copy-start(f32[24]{0:T(128)} %copy-done.27) | copy-start | bytes 292
  363.3 194.8 %copy-start.30 = (f32[24]{0:T(128)S(1)}, f32[24]{0:T(128)}, u32[]{:S(2)}) copy-start(f32[24]{0:T(128)} %copy-done.29) | copy-start | bytes 292
  363.3 216.2 %copy-start.33 = (f32[128]{0:T(128)S(1)}, f32[128]{0:T(128)}, u32[]{:S(2)}) copy-start(f32[128]{0:T(128)} %get-tuple-element.12) | copy-start | bytes 1540
  363.3 216.2 %copy-start.34 = (f32[128]{0:T(128)S(1)}, f32[128]{0:T(128)}, u32[]{:S(2)}) copy-start(f32[128]{0:T(128)} %get-tuple-element.10) | copy-start | bytes 1540
  363.4 278.2 %copy-start.25 = (bf16[24,768]{1,0:T(8,128)(2,1)S(1)}, bf16[24,768]{1,0:T(8,128)(2,1)}, u32[]{:S(2)}) copy-start(bf16[24,768]{1,0:T(8,128)(2,1)} %param.12) | copy-start | bytes 110596
  (20 other events, 27.3 us)
Sparse Core Ops, SparseCore 0:
  31.9 66.5 all-gather.2
  100.4 63.5 all-gather.4
  168.1 150.3 all-reduce.7
  329.8 110.6 reduce-scatter.4
  443.0 115.0 reduce-scatter.2
where the time goes:
time: 651 us; the launch traced here: 650 us
  waiting for transfers between devices  407 us (63%)
  blocking collectives  160 us (25%)
  matrix products  37.1 us (6%)
  other arithmetic  16.9 us (3%)
  local copies, waits for them, and re-layouts  14.4 us (2%)
  between operations  14.1 us (2%)
    reduce_scatter x1, waiting for transfers between devices, per_device(): lax.psum_scatter((contract_last(d_query, w_query) + contract_last(d_key,...  118 us
    psum x1, waiting for transfers between devices, per_device(): lax.psum((product(normed, w_query), product(normed, w_key), product(norme...  88.4 us
    reduce_scatter x1, waiting for transfers between devices, per_device(): lax.psum_scatter(contract_last(d_up, w_up).astype(jnp.bfloat16), 'wide',...  74.7 us
    all_gather x1, waiting for transfers between devices, per_device(): normed = lax.all_gather(own_normed, 'wide', axis=0, tiled=True)  66 us
    psum x1, blocking collectives, per_device(): lax.psum((gain_part, qgain_part, kgain_part), 'wide')  62 us
    all_gather x1, waiting for transfers between devices, per_device(): grad_rows = lax.all_gather(cotangent, 'wide', axis=0, tiled=True)  59.1 us
    psum x1, blocking collectives, per_device(): lax.psum((contract_last(grad_rows, w_out), contract_last(grad_rows, w_dow...  56.2 us
    psum x1, blocking collectives, per_device(): lax.psum((jnp.sum(as_float, axis=1), jnp.sum(as_float * as_float, axis=1)...  21.5 us
  transfers between devices with their start and end apart: 5, of which 5 were waited for; matrix products, arithmetic and copies ran while one was open for 7% of the time, Pallas kernels for 0%

commit v1 on v0

v1 whole, which is shorter than its diff:
```python
import functools
import math

import jax
import jax.numpy as jnp
from jax import lax
from jax.experimental import pallas as pl
from jax.experimental.pallas import tpu as pltpu
from jax.sharding import PartitionSpec as P

MESH = pl.DeviceIdType.MESH
F32 = jnp.float32
BF16 = jnp.bfloat16
EPS = 1e-06
PATCHES = 256
HEAD = 128
Z = 8
WIDE = 32
NARROW = 8
GELU_C = math.sqrt(2.0 / math.pi)
GELU_A = 0.044715


def nn(a, b):
    return lax.dot_general(a, b, (((1,), (0,)), ((), ())), preferred_element_type=F32)


def nt(a, b):
    return lax.dot_general(a, b, (((1,), (1,)), ((), ())), preferred_element_type=F32)


def tn(a, b):
    return lax.dot_general(a, b, (((0,), (0,)), ((), ())), preferred_element_type=F32)


def head_norm(matrix):
    centre = jnp.mean(matrix, axis=-1, keepdims=True)
    shifted = matrix - centre
    inv_std = lax.rsqrt(jnp.mean(shifted * shifted, axis=-1, keepdims=True) + EPS)
    return shifted * inv_std, inv_std


def norm_back(upstream, normal, inv_std):
    first = jnp.mean(upstream, axis=-1, keepdims=True)
    second = jnp.mean(upstream * normal, axis=-1, keepdims=True)
    return inv_std * (upstream - first - normal * second)


def gather_events():
    events = []
    for k in range(1, Z // 2):
        for d in range(2):
            for xs in range(2):
                events.append((2 + ((k - 1) * 2 + d) * 2 + xs, d, k, xs))
    return events


N_EVENTS = 2 + 4 * (Z // 2 - 1) + 2


def kernel(
    full_width,
    x_ref, cot_ref, ngain_ref, qgain_ref, kgain_ref,
    wq_hbm, wk_hbm, wv_hbm, wo_hbm, wu_hbm, wd_hbm,
    dx_ref, gq_ref, gk_ref, gv_ref, go_ref, gu_ref, gd_ref, gains_ref,
    wf, wdn,
    cg, ng, cf, nf,
    pd, pf, s1d, r1d, a1d, s2d, r2d, a2d, s3d, r3d,
    s1f, r1f, a1f, s2f, r2f, a2f, s3f, r3f,
    chunk_d, chunk_f,
    ga, gm, dqkv, att,
    dp, sc, rc, az, sz, rz, sx, rx,
    st, st2, gtile, gsib, gx, gz,
    wsem, ring_send, ring_recv, half_recv, sib_send, sib_recv, xp_send, xp_recv,
    rs_send, rs_recv, ag_send, ag_recv, st_send, st_recv,
    c_sem, z_send, z_recv, x_sem, g_sem, gz_send, gz_recv,
):
    w = lax.axis_index("wide")
    n = lax.axis_index("narrow")
    z = w // 4
    xl = (w // 2) % 2
    core = w % 2
    xh = n // 4
    y = n % 4
    zs = lambda k: (z + k + Z) % Z
    dev = lambda zz, xx, cc: zz * 4 + xx * 2 + cc

    bits = (((y + 1) // 2) % 2, y // 2, xh)
    cube = (
        (w, xh * 4 + y + 1 - 2 * (y % 2)),
        (w, xh * 4 + 3 - y),
        (w, (1 - xh) * 4 + y),
    )
    sibling = (dev(z, xl, 1 - core), n)
    xpartner = (dev(z, 1 - xl, core), n)
    z_next = ((dev(zs(1), xl, core), n), (dev(zs(-1), xl, core), n))
    z_peers = [(dev(zs(k), xl, core), n) for k in range(1, Z)]
    n_peers = [(w, (n + k) % NARROW) for k in range(1, NARROW)]

    pending = []

    def send(src, dst, ssem, rsem, to):
        copy = pltpu.make_async_remote_copy(
            src_ref=src, dst_ref=dst, send_sem=ssem, recv_sem=rsem, device_id=to, device_id_type=MESH
        )
        copy.start()
        pending.append(copy)
        return copy

    def recv(ref, ssem, rsem, frm):
        pltpu.make_async_remote_copy(
            src_ref=ref, dst_ref=ref, send_sem=ssem, recv_sem=rsem, device_id=frm, device_id_type=MESH
        ).wait_recv()

    wcopies = []
    for i, (src, dst) in enumerate((
        (wo_hbm, wdn.at[pl.ds(0, 128)]),
        (wd_hbm, wdn.at[pl.ds(128, 768)]),
        (wq_hbm, wf.at[:, pl.ds(0, 128)]),
        (wk_hbm, wf.at[:, pl.ds(128, 128)]),
        (wv_hbm, wf.at[:, pl.ds(256, 128)]),
        (wu_hbm, wf.at[:, pl.ds(384, 768)]),
    )):
        c = pltpu.make_async_copy(src, dst, wsem.at[i])
        c.start()
        wcopies.append(c)

    peers = [sibling, xpartner] + z_peers + n_peers
    barrier = pltpu.get_barrier_semaphore()
    for p in peers:
        pl.semaphore_signal(barrier, inc=1, device_id=p, device_id_type=MESH)
    pl.semaphore_wait(barrier, len(peers))

    half = cg.shape[-1] // 2

    def gather_own(g, i):
        slot = g.at[w]
        send(slot, slot, xp_send.at[i], xp_recv.at[i], xpartner)
        for d in range(2):
            send(slot, slot, ring_send.at[i, 0, d], ring_recv.at[i, 2 + d * 2], z_next[d])
        send(slot, slot, sib_send.at[i, 0], sib_recv.at[i, 0], sibling)

    def gather_partner(g, i):
        slot = g.at[dev(z, 1 - xl, core)]
        recv(slot, xp_send.at[i], xp_recv.at[i], xpartner)
        for d in range(2):
            send(slot, slot, ring_send.at[i, 1, d], ring_recv.at[i, 2 + d * 2 + 1], z_next[d])
        send(slot, slot, sib_send.at[i, 1], sib_recv.at[i, 1], sibling)

    def gather_step(g, i, k):
        for e, d, kk, xs in gather_events():
            if kk != k:
                continue
            x_at = xl if xs == 0 else 1 - xl
            slot = g.at[dev(zs(-k if d == 0 else k), x_at, core)]
            recv(slot, ring_send.at[i, e, d], ring_recv.at[i, e], z_next[1 - d])
            if k < Z // 2 - 1:
                send(slot, slot, ring_send.at[i, e, d], ring_recv.at[i, e + 4], z_next[d])
            else:
                part = slot.at[:, pl.ds(half * d, half)]
                send(part, part, ring_send.at[i, e, d], half_recv.at[i, d, xs], z_next[d])
            send(slot, slot, sib_send.at[i, e], sib_recv.at[i, e], sibling)

    def gather_far(g, i):
        for xs in range(2):
            x_at = xl if xs == 0 else 1 - xl
            slot = g.at[dev(zs(Z // 2), x_at, core)]
            e = N_EVENTS - 2 + xs
            for d in range(2):
                part = slot.at[:, pl.ds(half * d, half)]
                recv(part, ring_send.at[i, e, d], half_recv.at[i, d, xs], z_next[1 - d])
            send(slot, slot, sib_send.at[i, e], sib_recv.at[i, e], sibling)

    def gather_sibling(g, i):
        other = 1 - core
        recv(g.at[dev(z, xl, other)], sib_send.at[i, 0], sib_recv.at[i, 0], sibling)
        recv(g.at[dev(z, 1 - xl, other)], sib_send.at[i, 1], sib_recv.at[i, 1], sibling)
        for e, d, k, xs in gather_events():
            x_at = xl if xs == 0 else 1 - xl
            recv(g.at[dev(zs(-k if d == 0 else k), x_at, other)], sib_send.at[i, e], sib_recv.at[i, e], sibling)
        for xs in range(2):
            x_at = xl if xs == 0 else 1 - xl
            e = N_EVENTS - 2 + xs
            recv(g.at[dev(zs(Z // 2), x_at, other)], sib_send.at[i, e], sib_recv.at[i, e], sibling)

    def flatten(g, f):
        def body(p, _):
            both = jnp.concatenate([g[2 * p].astype(F32), g[2 * p + 1].astype(F32)], axis=0)
            f[pl.ds(pl.multiple_of(48 * p, 48), 48), :] = both.astype(BF16)
            return 0
        lax.fori_loop(0, WIDE // 2, body, 0)

    def small_sum(buf, j, a, b):
        lane = lax.broadcasted_iota(jnp.int32, (24, 128), 1)
        buf[n] = jnp.where(lane == 0, a, jnp.where(lane == 1, b, 0.0))
        for k, p in enumerate(n_peers):
            send(buf.at[n], buf.at[n], st_send.at[j, k], st_recv.at[j, k], p)

    def small_total(buf, j):
        for k in range(NARROW - 1):
            frm = (n - 1 - k + NARROW) % NARROW
            recv(buf.at[frm], st_send.at[j, k], st_recv.at[j, k], (w, frm))
        total = jnp.sum(buf[...], axis=0)
        return total[:, 0:1] / full_width, total[:, 1:2] / full_width

    cg[w] = cot_ref[...]
    gather_own(cg, 0)

    x = x_ref[...].astype(F32)
    small_sum(st, 0, jnp.sum(x, axis=1, keepdims=True), jnp.sum(x * x, axis=1, keepdims=True))
    gather_partner(cg, 0)
    row_mean, row_sq = small_total(st, 0)
    row_rstd = lax.rsqrt(row_sq - row_mean * row_mean + EPS)
    ng[w] = ((x_ref[...].astype(F32) - row_mean) * row_rstd * ngain_ref[...]).astype(BF16)
    gather_own(ng, 1)

    gather_step(cg, 0, 1)
    gather_partner(ng, 1)
    gather_step(cg, 0, 2)
    gather_step(ng, 1, 1)
    gather_step(cg, 0, 3)
    gather_step(ng, 1, 2)
    gather_far(cg, 0)
    gather_step(ng, 1, 3)
    gather_sibling(cg, 0)
    flatten(cg, cf)

    def at(ref, part, fixed):
        return ref.at[tuple(fixed.get(d, slice(None)) for d in range(3)) + (part,)]

    def rs_first(p, s1, r1, rnd):
        for r in range(3):
            s1[r] = at(p, r, {r: 1 - bits[r]})[...].astype(BF16)
            send(s1.at[r], r1.at[r], rs_send.at[rnd, 0, r], rs_recv.at[rnd, 0, r], cube[r])

    def rs_second(p, r1, a1, s2, r2, rnd):
        for r in range(3):
            e = (r + 1) % 3
            recv(r1.at[r], rs_send.at[rnd, 0, r], rs_recv.at[rnd, 0, r], cube[r])
            rest = [d for d in range(3) if d != r]
            pick = lambda v: tuple(v if d == e else slice(None) for d in rest)
            away, stay = 1 - bits[e], bits[e]
            s2[r] = (
                at(p, r, {r: bits[r], e: away})[...] + r1.at[(r,) + pick(away)][...].astype(F32)
            ).astype(BF16)
            send(s2.at[r], r2.at[r], rs_send.at[rnd, 1, r], rs_recv.at[rnd, 1, r], cube[e])
            a1[r] = at(p, r, {r: bits[r], e: stay})[...] + r1.at[(r,) + pick(stay)][...].astype(F32)

    def rs_third(r2, a1, s3, r3, a2, rnd):
        for r in range(3):
            e, f = (r + 1) % 3, (r + 2) % 3
            recv(r2.at[r], rs_send.at[rnd, 1, r], rs_recv.at[rnd, 1, r], cube[e])
            away, stay = 1 - bits[f], bits[f]
            s3[r] = (a1[r, away] + r2[r, away].astype(F32)).astype(BF16)
            send(s3.at[r], r3.at[r], rs_send.at[rnd, 2, r], rs_recv.at[rnd, 2, r], cube[f])
            a2[r] = a1[r, stay] + r2[r, stay].astype(F32)

    def rs_last(r3, a2, out, rnd):
        for r in range(3):
            f = (r + 2) % 3
            recv(r3.at[r], rs_send.at[rnd, 2, r], rs_recv.at[rnd, 2, r], cube[f])
            out[r] = a2[r] + r3[r].astype(F32)

    shape6 = lambda c: (2, 2, 2, 3, 32, c)

    wcopies[0].wait()
    wcopies[1].wait()
    pd[:, :, :, :, :, 0:128] = nt(cf[...], wdn[0:128, :]).reshape(shape6(128))
    for j in range(3):
        lo = 128 + 256 * j
        pd[:, :, :, :, :, lo:lo + 256] = nt(cf[...], wdn[lo:lo + 256, :]).reshape(shape6(256))
    rs_first(pd, s1d, r1d, 0)

    gather_far(ng, 1)
    gather_sibling(ng, 1)
    flatten(ng, nf)
    for c in wcopies[2:]:
        c.wait()
    for lo in range(0, 1152, 256):
        width = min(256, 1152 - lo)
        pf[:, :, :, :, :, lo:lo + width] = nn(nf[...], wf[:, lo:lo + width]).reshape(shape6(width))
    rs_first(pf, s1f, r1f, 1)

    rs_second(pd, r1d, a1d, s2d, r2d, 0)
    rs_second(pf, r1f, a1f, s2f, r2f, 1)
    rs_third(r2d, a1d, s3d, r3d, a2d, 0)
    rs_third(r2f, a1f, s3f, r3f, a2f, 1)
    rs_last(r3d, a2d, chunk_d, 0)
    rs_last(r3f, a2f, chunk_f, 1)

    def ag(buf, rnd, step):
        for r in range(3):
            order = ((r + 2) % 3, (r + 1) % 3, r)
            fixed = {d: bits[d] for d in order[step:]}
            src = at(buf, r, fixed)
            send(src, src, ag_send.at[rnd, step, r], ag_recv.at[rnd, step, r], cube[order[step]])

    def ag_wait(buf, rnd, step):
        for r in range(3):
            order = ((r + 2) % 3, (r + 1) % 3, r)
            fixed = {d: bits[d] for d in order[step:]}
            fixed[order[step]] = 1 - bits[order[step]]
            recv(at(buf, r, fixed), ag_send.at[rnd, step, r], ag_recv.at[rnd, step, r], cube[order[step]])

    mine = (bits[0], bits[1], bits[2])
    ga[mine + (slice(None), slice(None), pl.ds(0, 384))] = chunk_f[:, :, 0:384].astype(BF16)
    ga[mine + (slice(None), slice(None), pl.ds(384, 128))] = chunk_d[:, :, 0:128].astype(BF16)
    ag(ga, 0, 0)
    for r in range(3):
        up = chunk_f[r, :, 384:1152]
        dh = chunk_d[r, :, 128:896]
        sq = up * up
        t = jnp.tanh(GELU_C * up * (1.0 + GELU_A * sq))
        gm[mine + (r, slice(None), pl.ds(0, 768))] = (0.5 * up * (1.0 + t)).astype(BF16)
        slope = 0.5 * (1.0 + t) + 0.5 * up * (1.0 - t * t) * (GELU_C * (1.0 + 3.0 * GELU_A * sq))
        gm[mine + (r, slice(None), pl.ds(768, 768))] = (dh * slope).astype(BF16)
    ag(gm, 1, 0)
    ag_wait(ga, 0, 0)
    ag(ga, 0, 1)
    ag_wait(gm, 1, 0)
    ag(gm, 1, 1)
    ag_wait(ga, 0, 1)
    ag(ga, 0, 2)
    ag_wait(gm, 1, 1)
    ag(gm, 1, 2)
    ag_wait(ga, 0, 2)

    scale = HEAD ** (-0.5)
    qgain = qgain_ref[...]
    kgain = kgain_ref[...]
    qg = jnp.zeros((1, HEAD), F32)
    kg = jnp.zeros((1, HEAD), F32)
    for image in range(3):
        blocks = [(b // 3 // 4, b // 3 // 2 % 2, b // 3 % 2, b % 3) for b in range(image * 8, image * 8 + 8)]
        load = lambda lo: jnp.concatenate([ga[b + (slice(None), slice(lo, lo + 128))] for b in blocks], axis=0)
        q_unit, q_rstd = head_norm(load(0).astype(F32))
        k_unit, k_rstd = head_norm(load(128).astype(F32))
        values = load(256)
        d_att = load(384)
        q_normed = (q_unit * qgain).astype(BF16)
        k_normed = (k_unit * kgain).astype(BF16)
        exponent = jnp.exp(nt(q_normed, k_normed) * scale)
        probs = exponent / jnp.sum(exponent, axis=-1, keepdims=True)
        low = probs.astype(BF16)
        rows = slice(image * PATCHES, (image + 1) * PATCHES)
        att[rows, :] = nn(low, values).astype(BF16)
        d_probs = nt(d_att, values)
        dqkv[rows, 256:384] = tn(low, d_att).astype(BF16)
        d_scores = (probs * (d_probs - jnp.sum(probs * d_probs, axis=-1, keepdims=True))).astype(BF16)
        d_qnorm = nn(d_scores, k_normed) * scale
        d_knorm = tn(d_scores, q_normed) * scale
        qg = qg + jnp.sum(d_qnorm * q_unit, axis=0, keepdims=True)
        kg = kg + jnp.sum(d_knorm * k_unit, axis=0, keepdims=True)
        dqkv[rows, 0:128] = norm_back(d_qnorm * qgain, q_unit, q_rstd).astype(BF16)
        dqkv[rows, 128:256] = norm_back(d_knorm * kgain, k_unit, k_rstd).astype(BF16)

    go_ref[...] = tn(att[...], cf[...]).astype(BF16)
    for j in range(3):
        cols = slice(256 * j, 256 * j + 256)
        res = tn(nf[:, cols], dqkv[...]).astype(BF16)
        gq_ref[cols, :] = res[:, 0:128]
        gk_ref[cols, :] = res[:, 128:256]
        gv_ref[cols, :] = res[:, 256:384]

    ag_wait(gm, 1, 2)
    gain_rows = []
    for j in range(3):
        cols = slice(256 * j, 256 * j + 256)
        d_up = gm[:, :, :, :, :, 768:1536].reshape(768, 768)
        res = nt(dqkv[...], wf[cols, 0:384]) + nt(d_up, wf[cols, 384:1152])
        dp[:, :, :, :, cols] = res.reshape(Z, 2, 2, 24, 256)
        part = jnp.sum(res * nf[:, cols].astype(F32), axis=0, keepdims=True) / ngain_ref[:, cols]
        gain_rows += [part[:, 0:128], part[:, 128:256]]
    sc[...] = dp[:, :, pl.ds(1 - core, 1)].reshape(Z, 2, 24, 768).astype(BF16)
    core_copy = send(sc, rc, c_sem.at[0], c_sem.at[1], sibling)
    gtile[0] = jnp.concatenate(gain_rows + [qg, kg], axis=0)
    g_sib = send(gtile.at[0], gsib, g_sem.at[0], g_sem.at[1], sibling)

    core_copy.wait_recv()
    for k in range(1, Z):
        zz = zs(k)
        sz[k - 1] = (dp[zz, :, core] + rc[zz].astype(F32)).astype(BF16)
        send(sz.at[k - 1], rz.at[k - 1], z_send.at[k - 1], z_recv.at[k - 1], z_peers[k - 1])
    az[...] = dp[z, :, core] + rc[z].astype(F32)

    g_sib.wait_recv()
    gtile[1] = gtile[0] + gsib[...]
    g_xp = send(gtile.at[1], gx, g_sem.at[2], g_sem.at[3], xpartner)

    for j in range(3):
        cols = slice(256 * j, 256 * j + 256)
        d_up = gm[:, :, :, :, :, 768:1536].reshape(768, 768)
        gu_ref[cols, :] = tn(nf[:, cols], d_up).astype(BF16)
    g_xp.wait_recv()
    gtile[2] = gtile[1] + gx[...]
    for k in range(1, Z):
        send(gtile.at[2], gz.at[k - 1], gz_send.at[k - 1], gz_recv.at[k - 1], z_peers[k - 1])
    for j in range(3):
        cols = slice(256 * j, 256 * j + 256)
        hidden = gm[:, :, :, :, :, cols].reshape(768, 256)
        gd_ref[cols, :] = tn(hidden, cf[...]).astype(BF16)

    for k in range(1, Z):
        recv(rz.at[k - 1], z_send.at[k - 1], z_recv.at[k - 1], z_peers[Z - 1 - k])
        az[...] += rz[k - 1].astype(F32)
    sx[...] = az[1 - xl].astype(BF16)
    x_copy = send(sx, rx, x_sem.at[0], x_sem.at[1], xpartner)
    total = gtile[2]
    for k in range(1, Z):
        recv(gz.at[k - 1], gz_send.at[k - 1], gz_recv.at[k - 1], z_peers[Z - 1 - k])
        total = total + gz[k - 1]
    gains_ref[...] = total
    x_copy.wait_recv()
    d_unit = (az[xl] + rx[...].astype(F32)) * ngain_ref[...]
    unit = (x_ref[...].astype(F32) - row_mean) * row_rstd
    small_sum(st2, 1, jnp.sum(d_unit, axis=1, keepdims=True), jnp.sum(d_unit * unit, axis=1, keepdims=True))
    first, second = small_total(st2, 1)
    dx_ref[...] = (cot_ref[...].astype(F32) + row_rstd * (d_unit - first - unit * second)).astype(BF16)

    for c in pending:
        c.wait_send()


def per_device(inputs, cotangent, norm_gain, q_gain, k_gain, w_query, w_key, w_value, w_out, w_up, w_down):
    full_width = inputs.shape[1] * NARROW
    vm = pl.BlockSpec(memory_space=pltpu.VMEM)
    anywhere = pl.BlockSpec(memory_space=pl.ANY)
    v = pltpu.VMEM
    dma = pltpu.SemaphoreType.DMA

    def rs_buffers(c):
        return [
            v((3, 2, 2, 32, c), BF16), v((3, 2, 2, 32, c), BF16), v((3, 2, 32, c), F32),
            v((3, 2, 32, c), BF16), v((3, 2, 32, c), BF16), v((3, 32, c), F32),
            v((3, 32, c), BF16), v((3, 32, c), BF16),
        ]

    scratch = [
        v((768, 1152), BF16), v((896, 768), BF16),
        v((WIDE, 24, 768), BF16), v((WIDE, 24, 768), BF16), v((768, 768), BF16), v((768, 768), BF16),
        v((2, 2, 2, 3, 32, 896), F32), v((2, 2, 2, 3, 32, 1152), F32),
        *rs_buffers(896), *rs_buffers(1152),
        v((3, 32, 896), F32), v((3, 32, 1152), F32),
        v((2, 2, 2, 3, 32, 512), BF16), v((2, 2, 2, 3, 32, 1536), BF16), v((768, 384), BF16), v((768, 128), BF16),
        v((Z, 2, 2, 24, 768), F32), v((Z, 2, 24, 768), BF16), v((Z, 2, 24, 768), BF16), v((2, 24, 768), F32),
        v((Z - 1, 2, 24, 768), BF16), v((Z - 1, 2, 24, 768), BF16), v((24, 768), BF16), v((24, 768), BF16),
        v((NARROW, 24, 128), F32), v((NARROW, 24, 128), F32),
        v((3, 8, 128), F32), v((8, 128), F32), v((8, 128), F32), v((Z - 1, 8, 128), F32),
        dma((6,)), dma((2, N_EVENTS, 2)), dma((2, N_EVENTS)), dma((2, 2, 2)), dma((2, N_EVENTS)), dma((2, N_EVENTS)),
        dma((2,)), dma((2,)),
        dma((2, 3, 3)), dma((2, 3, 3)), dma((2, 3, 3)), dma((2, 3, 3)),
        dma((2, NARROW - 1)), dma((2, NARROW - 1)),
        dma((2,)), dma((Z - 1,)), dma((Z - 1,)), dma((2,)), dma((4,)), dma((Z - 1,)), dma((Z - 1,)),
    ]
    outs = pl.pallas_call(
        functools.partial(kernel, full_width),
        out_shape=(
            jax.ShapeDtypeStruct((24, 768), BF16),
            jax.ShapeDtypeStruct((768, 128), BF16),
            jax.ShapeDtypeStruct((768, 128), BF16),
            jax.ShapeDtypeStruct((768, 128), BF16),
            jax.ShapeDtypeStruct((128, 768), BF16),
            jax.ShapeDtypeStruct((768, 768), BF16),
            jax.ShapeDtypeStruct((768, 768), BF16),
            jax.ShapeDtypeStruct((8, 128), F32),
        ),
        in_specs=[vm] * 5 + [anywhere] * 6,
        out_specs=[vm] * 8,
        scratch_shapes=scratch,
        compiler_params=pltpu.CompilerParams(
            collective_id=0, has_side_effects=True, vmem_limit_bytes=60 * 1024 * 1024
        ),
    )(
        inputs, cotangent, norm_gain.reshape(1, -1), q_gain.reshape(1, -1), k_gain.reshape(1, -1),
        w_query, w_key, w_value, w_out, w_up, w_down,
    )
    gains = outs[7]
    return (*outs[:7], gains[:6].reshape(-1), gains[6], gains[7])


def solution(mesh):
    return jax.shard_map(
        per_device,
        mesh=mesh,
        in_specs=(
            P("wide", "narrow"), P("wide", "narrow"), P("narrow"), P(), P(),
            P("narrow", "wide"), P("narrow", "wide"), P("narrow", "wide"), P("wide", "narrow"),
            P("narrow", "wide"), P("wide", "narrow"),
        ),
        out_specs=(
            P("wide", "narrow"),
            P("narrow", "wide"), P("narrow", "wide"), P("narrow", "wide"), P("wide", "narrow"),
            P("narrow", "wide"), P("wide", "narrow"),
            P("narrow"), P(), P(),
        ),
        check_vma=False,
    )
```

time: 651 us -> 125 us (0.19)
  waiting for transfers between devices: 407 us -> 0 us
  blocking collectives: 160 us -> 0 us
  Pallas kernels: 0 us -> 109 us
  matrix products: 37.1 us -> 0 us
  other arithmetic: 16.9 us -> 0 us
  between operations: 14.1 us -> 0.66 us
    reduce_scatter x2 -> x0, waiting for transfers between devices: 192 us -> none  [the longest x1 118 us: per_device(): lax.psum_scatter((contract_last(d_query, w_query) + contract_last(d_key,...]
    psum x4 -> x0, blocking collectives: 160 us -> none  [the longest x1 62 us: per_device(): lax.psum((gain_part, qgain_part, kgain_part), 'wide')]
    all_gather x2 -> x0, waiting for transfers between devices: 125 us -> none  [the longest x1 66 us: per_device(): normed = lax.all_gather(own_normed, 'wide', axis=0, tiled=True)]
    pallas_call x0 -> x1, Pallas kernels: none -> 109 us  [per_device(): pl.pallas_call(functools.partial(kernel, full_width), out_shape=(jax.Shap...]
    psum x1 -> x0, waiting for transfers between devices: 88.4 us -> none  [per_device(): lax.psum((product(normed, w_query), product(normed, w_key), product(norme...]
    dot_general x21 -> x0, matrix products: 34.6 us -> none  [the longest x6 11.5 us: contract_last(): lax.dot_general(left, right, (((1,), (1,)), ((), ())), preferred_element_...]
    convert_element_type x6 -> x0, other arithmetic: 9.84 us -> none  [the longest x1 3.94 us: per_device(): d_up = gelu_pull(d_hidden)[0].astype(jnp.bfloat16)]
  transfers between devices with their start and end apart: 5 -> 0, of which waited for: 5 -> 0; matrix products, arithmetic and copies ran while one was open for 7% -> 0% of each run, Pallas kernels for 0% -> 0%
where the time goes in v1:
time: 125 us; the launch traced here: 124 us
  Pallas kernels  109 us (87%)
  local copies, waits for them, and re-layouts  14.5 us (12%)
    pallas_call x1, Pallas kernels, per_device(): pl.pallas_call(functools.partial(kernel, full_width), out_shape=(jax.Shap...  109 us
    unnamed x11, local copies, waits for them, and re-layouts  10.6 us

profile of v1, /device:TPU:1, one launch (start us, length us, event | category | flops | bytes accessed | tf_op | source)
XLA Modules:
  0.0 124.4 jit_solution(402341015369615702)
XLA Ops:
  0.6 1.3 %reshape.32.ngain_ref = f32[1,768]{1,0:T(1,128)} reshape(f32[768]{0:T(1024)} %param.13) | data formatting | bytes 6144 | tf_op jit(solution)/shard_map/reshape | solution.py:474
  1.9 109.3 %shard_map.186 = (bf16[24,768]{1,0:T(8,128)(2,1)}, bf16[768,128]{1,0:T(8,128)(2,1)}, bf16[768,128]{1,0:T(8,128)(2,1)}, bf16[768,128]{1,0:T(8,128)(2,1)}, bf16[12...) custom-call(bf16[24,768]{1,0:T(8,128)(2,1)} %x_ref.1, ...), custom_call_target="tpu_custom_call" | custom-call | tf_op jit(solution)/shard_map/pallas_call | solution.py:455
  111.2 0.0 copy-start.1
  111.2 1.4 %slice_bitcast_fusion = f32[768]{0:T(1024)} fusion(f32[8,128]{1,0:T(8,128)} %get-tuple-element.25), kind=kLoop, calls=%fused_computation | loop fusion | bytes 6144 | tf_op jit(solution)/shard_map/reshape | solution.py:478
  112.6 1.3 %slice_bitcast_fusion.1 = (f32[128]{0:T(128)}, f32[128]{0:T(128)}) fusion(f32[8,128]{1,0:T(8,128)} %get-tuple-element.25), kind=kLoop, calls=%fused_computation.1 | loop fusion | bytes 2048 | tf_op jit(solution)/shard_map/squeeze | solution.py:478
  113.8 1.4 %copy.28 = bf16[24,768]{1,0:T(8,128)(2,1)} copy(bf16[24,768]{1,0:T(8,128)(2,1)} %get-tuple-element.38) | data formatting | bytes 73728
  115.2 1.6 %copy.29 = bf16[768,128]{1,0:T(8,128)(2,1)} copy(bf16[768,128]{1,0:T(8,128)(2,1)} %get-tuple-element.39) | data formatting | bytes 393216
  116.8 1.6 %copy.30 = bf16[768,128]{1,0:T(8,128)(2,1)} copy(bf16[768,128]{1,0:T(8,128)(2,1)} %get-tuple-element.40) | data formatting | bytes 393216
  118.4 1.6 %copy.31 = bf16[768,128]{1,0:T(8,128)(2,1)} copy(bf16[768,128]{1,0:T(8,128)(2,1)} %get-tuple-element.41) | data formatting | bytes 393216
  120.0 1.6 %copy.32 = bf16[128,768]{1,0:T(8,128)(2,1)} copy(bf16[128,768]{1,0:T(8,128)(2,1)} %get-tuple-element.42) | data formatting | bytes 393216
  121.7 0.0 copy-done.1
  121.7 0.0 copy-start
  121.7 1.0 copy.33
  122.7 0.7 copy-done
  123.4 1.0 copy.34
Async XLA Ops:
  111.2 10.5 %copy-start.1 = (bf16[768,768]{1,0:T(8,128)(2,1)S(1)}, bf16[768,768]{1,0:T(8,128)(2,1)}, u32[]{:S(2)}) copy-start(bf16[768,768]{1,0:T(8,128)(2,1)} %get-tuple-element.43) | copy-start | bytes 3538948
  121.7 1.7 %copy-start = (bf16[768,768]{1,0:T(8,128)(2,1)S(1)}, bf16[768,768]{1,0:T(8,128)(2,1)}, u32[]{:S(2)}) copy-start(bf16[768,768]{1,0:T(8,128)(2,1)} %get-tuple-element.44) | copy-start | bytes 3538948

commit v2 on v1

v2 whole, which is shorter than its diff:
```python
import functools
import math

import jax
import jax.numpy as jnp
from jax import lax
from jax.experimental import pallas as pl
from jax.experimental.pallas import tpu as pltpu
from jax.sharding import PartitionSpec as P

MESH = pl.DeviceIdType.MESH
F32 = jnp.float32
BF16 = jnp.bfloat16
EPS = 1e-06
PATCHES = 256
HEAD = 128
Z = 8
FAR = Z // 2
WIDE = 32
NARROW = 8
GELU_C = math.sqrt(2.0 / math.pi)
GELU_A = 0.044715


def nn(a, b):
    return lax.dot_general(a, b, (((1,), (0,)), ((), ())), preferred_element_type=F32)


def nt(a, b):
    return lax.dot_general(a, b, (((1,), (1,)), ((), ())), preferred_element_type=F32)


def tn(a, b):
    return lax.dot_general(a, b, (((0,), (0,)), ((), ())), preferred_element_type=F32)


def head_norm(matrix):
    centre = jnp.mean(matrix, axis=-1, keepdims=True)
    shifted = matrix - centre
    inv_std = lax.rsqrt(jnp.mean(shifted * shifted, axis=-1, keepdims=True) + EPS)
    return shifted * inv_std, inv_std


def norm_back(upstream, normal, inv_std):
    first = jnp.mean(upstream, axis=-1, keepdims=True)
    second = jnp.mean(upstream * normal, axis=-1, keepdims=True)
    return inv_std * (upstream - first - normal * second)


def kernel(
    full_width,
    x_ref, cot_ref, ngain_ref, qgain_ref, kgain_ref,
    wq_hbm, wk_hbm, wv_hbm, wo_hbm, wu_hbm, wd_hbm,
    dx, gq, gk, gv, go, gu, gd, gains,
    wf, wdn,
    cg, ng, cf, nf,
    pd, pq, pu,
    bde, bdl, bq, bul, bue,
    ga, gp, gh, dqkv, att,
    dp, sib_s, sib_r, x_s, x_r, z_s, z_r, fin, fin_s, fin_r,
    st, st2, gtile, gquad, gz,
    wsem, sib_send, sib_recv, xp_send, xp_recv, line_send, line_recv,
    rs_send, rs_recv, ag_send, ag_recv, st_send, st_recv,
    c_sem, x_sem, z_send, z_recv, f_sem, gq_send, gq_recv, gz_send, gz_recv,
):
    w = lax.axis_index("wide")
    n = lax.axis_index("narrow")
    z = w // 4
    xl = (w // 2) % 2
    core = w % 2
    xh = n // 4
    y = n % 4
    way = 1 - 2 * core
    zs = lambda k: (z + k + Z) % Z
    dev = lambda zz, xx, cc: zz * 4 + xx * 2 + cc

    bits = (((y + 1) // 2) % 2, y // 2, xh)
    cube = (
        (w, xh * 4 + y + 1 - 2 * (y % 2)),
        (w, xh * 4 + 3 - y),
        (w, (1 - xh) * 4 + y),
    )
    sibling = (dev(z, xl, 1 - core), n)
    quad = (sibling, (dev(z, 1 - xl, core), n), (dev(z, 1 - xl, 1 - core), n))
    quad_at = ((xl, 1 - core), (1 - xl, core), (1 - xl, 1 - core))
    xpartner = quad[1]
    z_peers = [(dev(zs(k), xl, core), n) for k in range(1, Z)]
    n_peers = [(w, (n + k) % NARROW) for k in range(1, NARROW)]

    pending = []

    def send(src, dst, ssem, rsem, to):
        copy = pltpu.make_async_remote_copy(
            src_ref=src, dst_ref=dst, send_sem=ssem, recv_sem=rsem, device_id=to, device_id_type=MESH
        )
        copy.start()
        pending.append(copy)

    def recv(ref, ssem, rsem, frm):
        pltpu.make_async_remote_copy(
            src_ref=ref, dst_ref=ref, send_sem=ssem, recv_sem=rsem, device_id=frm, device_id_type=MESH
        ).wait_recv()

    wcopies = []
    for i, (src, dst) in enumerate((
        (wo_hbm, wdn.at[pl.ds(0, 128)]),
        (wd_hbm, wdn.at[pl.ds(128, 768)]),
        (wq_hbm, wf.at[:, pl.ds(0, 128)]),
        (wk_hbm, wf.at[:, pl.ds(128, 128)]),
        (wv_hbm, wf.at[:, pl.ds(256, 128)]),
        (wu_hbm, wf.at[:, pl.ds(384, 768)]),
    )):
        c = pltpu.make_async_copy(src, dst, wsem.at[i])
        c.start()
        wcopies.append(c)

    peers = [*quad, *z_peers, *n_peers]
    barrier = pltpu.get_barrier_semaphore()
    for p in peers:
        pl.semaphore_signal(barrier, inc=1, device_id=p, device_id_type=MESH)
    ngain = jnp.concatenate([ngain_ref[pl.ds(128 * i, 128)].reshape(1, 128) for i in range(6)], axis=1)
    cg[z, xl, core] = cot_ref[...]
    pl.semaphore_wait(barrier, len(peers))

    def gather_own(g, i):
        slot = g.at[z, xl, core]
        send(slot, slot, sib_send.at[i, 0], sib_recv.at[i, 0], sibling)
        send(slot, slot, xp_send.at[i, 0], xp_recv.at[i, 0], xpartner)

    def gather_out(g, i):
        recv(g.at[z, xl, 1 - core], sib_send.at[i, 0], sib_recv.at[i, 0], sibling)
        for k in range(1, FAR + 1):
            slot = g.at[z, xl] if k < FAR else g.at[z, xl, core]
            send(slot, slot, line_send.at[i, k], line_recv.at[i, k], (dev(zs(way * k), xl, core), n))

    def gather_line(g, i, k):
        zz = zs(-way * k)
        slot = g.at[zz, xl] if k < FAR else g.at[zz, xl, core]
        recv(slot, line_send.at[i, k], line_recv.at[i, k], (dev(zz, xl, core), n))
        send(slot, slot, sib_send.at[i, k], sib_recv.at[i, k], sibling)
        send(slot, slot, xp_send.at[i, k], xp_recv.at[i, k], xpartner)

    def gather_x(g, i, k):
        zz = zs(-way * k)
        slot = g.at[zz, 1 - xl] if 0 < k < FAR else g.at[zz, 1 - xl, core]
        recv(slot, xp_send.at[i, k], xp_recv.at[i, k], xpartner)
        send(slot, slot, sib_send.at[i, FAR + 1 + k], sib_recv.at[i, FAR + 1 + k], sibling)

    def flatten(g, f, xx, zz):
        block = jnp.concatenate([g[zz, xx, 0].astype(F32), g[zz, xx, 1].astype(F32)], axis=0)
        f[xx, pl.ds(pl.multiple_of(48 * zz, 48), 48), :] = block.astype(BF16)

    def flatten_own(g, i, f, k):
        zz = zs(way * k)
        if k > 0:
            slot = g.at[zz, xl] if k < FAR else g.at[zz, xl, 1 - core]
            recv(slot, sib_send.at[i, k], sib_recv.at[i, k], sibling)
        flatten(g, f, xl, zz)
        if 0 < k < FAR:
            flatten(g, f, xl, zs(-way * k))

    def flatten_partner(g, i, f, k):
        zz = zs(way * k)
        slot = g.at[zz, 1 - xl] if 0 < k < FAR else g.at[zz, 1 - xl, 1 - core]
        recv(slot, sib_send.at[i, FAR + 1 + k], sib_recv.at[i, FAR + 1 + k], sibling)
        flatten(g, f, 1 - xl, zz)
        if 0 < k < FAR:
            flatten(g, f, 1 - xl, zs(-way * k))

    def small_sum(buf, j, a, b):
        lane = lax.broadcasted_iota(jnp.int32, (24, 128), 1)
        buf[n] = jnp.where(lane == 0, a, jnp.where(lane == 1, b, 0.0))
        for k, p in enumerate(n_peers):
            send(buf.at[n], buf.at[n], st_send.at[j, k], st_recv.at[j, k], p)

    def small_total(buf, j):
        for k in range(NARROW - 1):
            frm = (n - 1 - k + NARROW) % NARROW
            recv(buf.at[frm], st_send.at[j, k], st_recv.at[j, k], (w, frm))
        total = jnp.sum(buf[...], axis=0)
        return total[:, 0:1] / full_width, total[:, 1:2] / full_width

    gather_own(cg, 0)
    x = x_ref[...].astype(F32)
    small_sum(st, 0, jnp.sum(x, axis=1, keepdims=True), jnp.sum(x * x, axis=1, keepdims=True))
    gather_out(cg, 0)
    row_mean, row_sq = small_total(st, 0)
    row_rstd = lax.rsqrt(row_sq - row_mean * row_mean + EPS)
    ng[z, xl, core] = ((x_ref[...].astype(F32) - row_mean) * row_rstd * ngain).astype(BF16)
    gather_own(ng, 1)

    every = slice(None)

    def at(ref, half, part, fixed):
        return ref.at[(half,) + tuple(fixed.get(d, every) for d in range(3)) + (part,)]

    def lead(half):
        return (every,) if half is every else ()

    def rs_first(p, half, b, rnd):
        s1, r1 = b[0], b[1]
        for r in range(3):
            s1[r] = at(p, half, r, {r: 1 - bits[r]})[...].astype(BF16)
            send(s1.at[r], r1.at[r], rs_send.at[rnd, 0, r], rs_recv.at[rnd, 0, r], cube[r])

    def rs_second(p, half, b, rnd):
        r1, a1, s2, r2 = b[1:5]
        for r in range(3):
            e = (r + 1) % 3
            recv(r1.at[r], rs_send.at[rnd, 0, r], rs_recv.at[rnd, 0, r], cube[r])
            rest = [d for d in range(3) if d != r]
            pick = lambda v: (r,) + lead(half) + tuple(v if d == e else every for d in rest)
            away, stay = 1 - bits[e], bits[e]
            s2[r] = (
                at(p, half, r, {r: bits[r], e: away})[...] + r1.at[pick(away)][...].astype(F32)
            ).astype(BF16)
            send(s2.at[r], r2.at[r], rs_send.at[rnd, 1, r], rs_recv.at[rnd, 1, r], cube[e])
            a1[r] = at(p, half, r, {r: bits[r], e: stay})[...] + r1.at[pick(stay)][...].astype(F32)

    def rs_third(half, b, rnd):
        a1, r2, a2, s3, r3 = b[2], b[4], b[5], b[6], b[7]
        for r in range(3):
            e, f = (r + 1) % 3, (r + 2) % 3
            recv(r2.at[r], rs_send.at[rnd, 1, r], rs_recv.at[rnd, 1, r], cube[e])
            away, stay = (r,) + lead(half) + (1 - bits[f],), (r,) + lead(half) + (bits[f],)
            s3[r] = (a1[away] + r2[away].astype(F32)).astype(BF16)
            send(s3.at[r], r3.at[r], rs_send.at[rnd, 2, r], rs_recv.at[rnd, 2, r], cube[f])
            a2[r] = a1[stay] + r2[stay].astype(F32)

    def rs_last(b, rnd):
        a2, r3 = b[5], b[7]
        for r in range(3):
            f = (r + 2) % 3
            recv(r3.at[r], rs_send.at[rnd, 2, r], rs_recv.at[rnd, 2, r], cube[f])
            a2[r] = a2[r] + r3[r].astype(F32)

    def cot_products(half):
        lhs = lambda: cf[half]
        shape = lambda c: (2, 2, 2, 3, 16, c)
        pd[half, :, :, :, :, :, 0:128] = nt(lhs(), wdn[0:128, :]).reshape(shape(128))
        for j in range(3):
            lo = 128 + 256 * j
            pd[half, :, :, :, :, :, lo:lo + 256] = nt(lhs(), wdn[lo:lo + 256, :]).reshape(shape(256))

    def ag(buf, half, rnd, step):
        for r in range(3):
            order = ((r + 2) % 3, (r + 1) % 3, r)
            src = at(buf, half, r, {d: bits[d] for d in order[step:]})
            send(src, src, ag_send.at[rnd, step, r], ag_recv.at[rnd, step, r], cube[order[step]])

    def ag_wait(buf, half, rnd, step):
        for r in range(3):
            order = ((r + 2) % 3, (r + 1) % 3, r)
            fixed = {d: bits[d] for d in order[step:]}
            fixed[order[step]] = 1 - bits[order[step]]
            recv(
                at(buf, half, r, fixed), ag_send.at[rnd, step, r], ag_recv.at[rnd, step, r], cube[order[step]]
            )

    mine = (bits[0], bits[1], bits[2])
    theirs = 1 - xl

    def gelu(half, b_up, b_d):
        up = b_up[5][...]
        sq = up * up
        t = jnp.tanh(GELU_C * up * (1.0 + GELU_A * sq))
        gh[(half,) + mine] = (0.5 * up * (1.0 + t)).astype(BF16)
        slope = 0.5 * (1.0 + t) + 0.5 * up * (1.0 - t * t) * (GELU_C * (1.0 + 3.0 * GELU_A * sq))
        gp[(half,) + mine] = (b_d[5][:, :, 128:896] * slope).astype(BF16)

    gather_line(cg, 0, 1)
    gather_line(cg, 0, 2)
    gather_out(ng, 1)
    gather_x(cg, 0, 0)
    gather_line(cg, 0, 3)
    gather_x(cg, 0, 1)
    gather_line(cg, 0, 4)
    flatten_own(cg, 0, cf, 0)
    flatten_own(cg, 0, cf, 1)
    gather_x(cg, 0, 2)
    flatten_own(cg, 0, cf, 2)
    flatten_own(cg, 0, cf, 3)
    flatten_own(cg, 0, cf, 4)
    wcopies[0].wait()
    wcopies[1].wait()
    cot_products(xl)
    rs_first(pd, xl, bde, 0)

    gather_x(cg, 0, 3)
    gather_line(ng, 1, 1)
    gather_x(cg, 0, 4)
    gather_line(ng, 1, 2)
    gather_x(ng, 1, 0)
    for k in range(FAR + 1):
        flatten_partner(cg, 0, cf, k)
    gather_line(ng, 1, 3)
    gather_x(ng, 1, 1)
    gather_line(ng, 1, 4)
    cot_products(theirs)
    rs_first(pd, theirs, bdl, 1)

    gather_x(ng, 1, 2)
    flatten_own(ng, 1, nf, 0)
    flatten_own(ng, 1, nf, 1)
    flatten_own(ng, 1, nf, 2)
    gather_x(ng, 1, 3)
    flatten_own(ng, 1, nf, 3)
    flatten_own(ng, 1, nf, 4)
    gather_x(ng, 1, 4)
    rs_second(pd, xl, bde, 0)
    for k in range(FAR + 1):
        flatten_partner(ng, 1, nf, k)
    for c in wcopies[2:]:
        c.wait()
    lhs = lambda: nf[...].reshape(768, 768)
    shape = lambda c: (2, 2, 2, 2, 3, 16, c)
    pq[:, :, :, :, :, :, 0:256] = nn(lhs(), wf[:, 0:256]).reshape(shape(256))
    pq[:, :, :, :, :, :, 256:384] = nn(lhs(), wf[:, 256:384]).reshape(shape(128))
    rs_first(pq, every, bq, 2)
    rs_second(pd, theirs, bdl, 1)
    for j in range(3):
        lo = 256 * j
        pu[:, :, :, :, :, :, lo:lo + 256] = nn(lhs(), wf[:, 384 + lo:640 + lo]).reshape(shape(256))
    rs_first(pu, theirs, bul, 3)
    rs_first(pu, xl, bue, 4)

    rs_third(xl, bde, 0)
    rs_second(pq, every, bq, 2)
    rs_third(theirs, bdl, 1)
    rs_second(pu, theirs, bul, 3)
    rs_last(bde, 0)
    rs_third(every, bq, 2)
    rs_last(bdl, 1)
    rs_second(pu, xl, bue, 4)
    rs_last(bq, 2)
    for r in range(3):
        ga[(every,) + mine + (r, every, pl.ds(0, 384))] = bq[5][r].astype(BF16)
    ga[(xl,) + mine + (every, every, pl.ds(384, 128))] = bde[5][:, :, 0:128].astype(BF16)
    ga[(theirs,) + mine + (every, every, pl.ds(384, 128))] = bdl[5][:, :, 0:128].astype(BF16)
    ag(ga, every, 0, 0)
    rs_third(theirs, bul, 3)
    rs_third(xl, bue, 4)
    ag_wait(ga, every, 0, 0)
    ag(ga, every, 0, 1)
    rs_last(bul, 3)
    gelu(theirs, bul, bdl)
    ag(gp, theirs, 1, 0)
    rs_last(bue, 4)
    gelu(xl, bue, bde)
    ag(gp, xl, 2, 0)
    ag_wait(ga, every, 0, 1)
    ag(ga, every, 0, 2)
    ag_wait(gp, theirs, 1, 0)
    ag(gp, theirs, 1, 1)
    ag(gh, every, 3, 0)
    ag_wait(gp, xl, 2, 0)
    ag(gp, xl, 2, 1)
    ag_wait(ga, every, 0, 2)

    scale = HEAD ** (-0.5)
    qgain = qgain_ref[...]
    kgain = kgain_ref[...]
    gain_sums = [jnp.zeros((1, HEAD), F32), jnp.zeros((1, HEAD), F32)]

    def attention(image):
        places = [(b % 6 // 3, b // 6, b % 3) for b in range(image * 16, image * 16 + 16)]
        load = lambda lo: jnp.concatenate(
            [ga[xx, c // 4, c // 2 % 2, c % 2, r, :, lo:lo + 128] for xx, c, r in places], axis=0
        )

        def store(ref, lo, value):
            for i, (xx, c, r) in enumerate(places):
                ref[xx, c, r, :, lo:lo + 128] = value[16 * i:16 * i + 16]

        q_unit, q_rstd = head_norm(load(0).astype(F32))
        k_unit, k_rstd = head_norm(load(128).astype(F32))
        values = load(256)
        d_att = load(384)
        q_normed = (q_unit * qgain).astype(BF16)
        k_normed = (k_unit * kgain).astype(BF16)
        exponent = jnp.exp(nt(q_normed, k_normed) * scale)
        probs = exponent / jnp.sum(exponent, axis=-1, keepdims=True)
        low = probs.astype(BF16)
        store(att, 0, nn(low, values).astype(BF16))
        d_probs = nt(d_att, values)
        store(dqkv, 256, tn(low, d_att).astype(BF16))
        d_scores = (probs * (d_probs - jnp.sum(probs * d_probs, axis=-1, keepdims=True))).astype(BF16)
        d_qnorm = nn(d_scores, k_normed) * scale
        d_knorm = tn(d_scores, q_normed) * scale
        gain_sums[0] = gain_sums[0] + jnp.sum(d_qnorm * q_unit, axis=0, keepdims=True)
        gain_sums[1] = gain_sums[1] + jnp.sum(d_knorm * k_unit, axis=0, keepdims=True)
        store(dqkv, 0, norm_back(d_qnorm * qgain, q_unit, q_rstd).astype(BF16))
        store(dqkv, 128, norm_back(d_knorm * kgain, k_unit, k_rstd).astype(BF16))

    attention(0)
    ag_wait(gp, theirs, 1, 1)
    ag(gp, theirs, 1, 2)
    ag_wait(gh, every, 3, 0)
    ag(gh, every, 3, 1)
    attention(1)
    ag_wait(gp, xl, 2, 1)
    ag(gp, xl, 2, 2)
    attention(2)

    gain_rows = []

    def products(half, e):
        d_heads = lambda: dqkv[half].reshape(384, 384)
        d_up = lambda: gp[half].reshape(384, 768)
        for j in range(3):
            cols = slice(256 * j, 256 * j + 256)
            res = nt(d_heads(), wf[cols, 0:384]) + nt(d_up(), wf[cols, 384:1152])
            dp[e, :, :, :, cols] = res.reshape(Z, 2, 24, 256)
            part = jnp.sum(res * nf[half, :, cols].astype(F32), axis=0, keepdims=True) / ngain[:, cols]
            gain_rows.append(part)
        for k in range(1, FAR):
            sib_s[e, k - 1] = dp[e, zs(-way * k)].astype(BF16)
        sib_s[e, FAR - 1, 0] = dp[e, zs(FAR), 1 - core].astype(BF16)
        sib_s[e, FAR - 1, 1] = dp[e, z, 1 - core].astype(BF16)
        send(sib_s.at[e], sib_r.at[e], c_sem.at[e, 0], c_sem.at[e, 1], sibling)

    def pair(e, k):
        return dp[e, zs(way * k)] + sib_r[e, k - 1].astype(F32)

    def far(e):
        return dp[e, zs(FAR), core] + sib_r[e, FAR - 1, 0].astype(F32)

    def near(e):
        return dp[e, z, core] + sib_r[e, FAR - 1, 1].astype(F32)

    ag_wait(gp, theirs, 1, 2)
    products(theirs, 0)
    ag_wait(gh, every, 3, 1)
    recv(sib_r.at[0], c_sem.at[0, 0], c_sem.at[0, 1], sibling)
    for k in range(1, FAR):
        x_s[k - 1] = pair(0, k).astype(BF16)
    x_s[FAR - 1, 0] = far(0).astype(BF16)
    x_s[FAR - 1, 1] = near(0).astype(BF16)
    send(x_s, x_r, x_sem.at[0], x_sem.at[1], xpartner)

    ag_wait(gp, xl, 2, 2)
    ag(gh, every, 3, 2)
    products(xl, 1)
    gain_rows = [
        (gain_rows[j] + gain_rows[j + 3])[:, 128 * i:128 * i + 128] for j in range(3) for i in range(2)
    ]
    gtile[0] = jnp.concatenate(gain_rows + gain_sums, axis=0)
    for j in range(3):
        send(gtile.at[0], gquad.at[j], gq_send.at[j], gq_recv.at[j], quad[j])
    recv(x_r, x_sem.at[0], x_sem.at[1], xpartner)
    recv(sib_r.at[1], c_sem.at[1, 0], c_sem.at[1, 1], sibling)
    for k in range(FAR - 1, 0, -1):
        z_s[k - 1] = (pair(1, k) + x_r[k - 1].astype(F32)).astype(BF16)
        send(z_s.at[k - 1], z_r.at[k - 1], z_send.at[k], z_recv.at[k], (dev(zs(way * k), xl, core), n))
    z_s[FAR - 1, 0] = (far(1) + x_r[FAR - 1, 0].astype(F32)).astype(BF16)
    send(
        z_s.at[FAR - 1, 0], z_r.at[FAR - 1, 0], z_send.at[FAR], z_recv.at[FAR], (dev(zs(FAR), xl, core), n)
    )
    fin[core] = near(1) + x_r[FAR - 1, 1].astype(F32)
    for j in range(3):
        recv(gquad.at[j], gq_send.at[j], gq_recv.at[j], quad[j])
    gtile[1] = gtile[0] + gquad[0] + gquad[1] + gquad[2]
    for k in range(1, Z):
        send(gtile.at[1], gz.at[k - 1], gz_send.at[k - 1], gz_recv.at[k - 1], z_peers[k - 1])

    for j in range(3):
        cols = slice(256 * j, 256 * j + 256)
        left = nf[:, :, cols].reshape(768, 256)
        gu[cols, :] = tn(left, gp[...].reshape(768, 768)).astype(BF16)
        res = tn(left, dqkv[...].reshape(768, 384)).astype(BF16)
        gq[cols, :] = res[:, 0:128]
        gk[cols, :] = res[:, 128:256]
        gv[cols, :] = res[:, 256:384]

    recv(z_r.at[FAR - 1, 0], z_send.at[FAR], z_recv.at[FAR], (dev(zs(FAR), xl, core), n))
    for k in range(1, FAR):
        recv(z_r.at[k - 1], z_send.at[k], z_recv.at[k], (dev(zs(-way * k), xl, core), n))
    fin[1 - core] = sum(z_r[k, 1 - core].astype(F32) for k in range(FAR - 1))
    fin_s[...] = fin[1 - core].astype(BF16)
    send(fin_s, fin_r, f_sem.at[0], f_sem.at[1], sibling)

    go[...] = tn(att[...].reshape(768, 128), cf[...].reshape(768, 768)).astype(BF16)

    d_own = fin[core] + z_r[FAR - 1, 0].astype(F32) + sum(z_r[k, core].astype(F32) for k in range(FAR - 1))
    recv(fin_r, f_sem.at[0], f_sem.at[1], sibling)
    d_normed = d_own + fin_r[...].astype(F32)
    d_unit = d_normed * ngain
    unit = (x_ref[...].astype(F32) - row_mean) * row_rstd
    small_sum(st2, 1, jnp.sum(d_unit, axis=1, keepdims=True), jnp.sum(d_unit * unit, axis=1, keepdims=True))

    ag_wait(gh, every, 3, 2)
    for j in range(3):
        cols = slice(256 * j, 256 * j + 256)
        hidden = gh[:, :, :, :, :, :, cols].reshape(768, 256)
        gd[cols, :] = tn(hidden, cf[...].reshape(768, 768)).astype(BF16)
    total = gtile[1]
    for k in range(1, Z):
        recv(gz.at[k - 1], gz_send.at[k - 1], gz_recv.at[k - 1], z_peers[Z - 1 - k])
        total = total + gz[k - 1]
    gains[...] = total

    first, second = small_total(st2, 1)
    dx[...] = (cot_ref[...].astype(F32) + row_rstd * (d_unit - first - unit * second)).astype(BF16)

    for c in pending:
        c.wait_send()


def hand_over(*refs):
    srcs, gains_ref, outs, (ngain_ref, qg_ref, kg_ref), sem = refs[:7], refs[7], refs[8:15], refs[15:18], refs[18]
    copies = [pltpu.make_async_copy(s, o, sem.at[i]) for i, (s, o) in enumerate(zip(srcs, outs))]
    for c in copies:
        c.start()
    for i in range(6):
        ngain_ref[pl.ds(128 * i, 128)] = gains_ref[i, :]
    qg_ref[...] = gains_ref[6, :]
    kg_ref[...] = gains_ref[7, :]
    for c in copies:
        c.wait()


def per_device(inputs, cotangent, norm_gain, q_gain, k_gain, w_query, w_key, w_value, w_out, w_up, w_down):
    full_width = inputs.shape[1] * NARROW
    vm = pl.BlockSpec(memory_space=pltpu.VMEM)
    anywhere = pl.BlockSpec(memory_space=pl.ANY)
    v = pltpu.VMEM
    dma = pltpu.SemaphoreType.DMA

    def rs_buffers(c, lead=()):
        return [
            v((3, *lead, 2, 2, 16, c), BF16), v((3, *lead, 2, 2, 16, c), BF16), v((3, *lead, 2, 16, c), F32),
            v((3, *lead, 2, 16, c), BF16), v((3, *lead, 2, 16, c), BF16), v((3, *lead, 16, c), F32),
            v((3, *lead, 16, c), BF16), v((3, *lead, 16, c), BF16),
        ]

    grads = [(24, 768), (768, 128), (768, 128), (768, 128), (128, 768), (768, 768), (768, 768)]
    cube = (2, 2, 2, 2, 3, 16)
    scratch = [
        v((768, 1152), BF16), v((896, 768), BF16),
        v((Z, 2, 2, 24, 768), BF16), v((Z, 2, 2, 24, 768), BF16), v((2, 384, 768), BF16), v((2, 384, 768), BF16),
        v((*cube, 896), F32), v((*cube, 384), F32), v((*cube, 768), F32),
        rs_buffers(896), rs_buffers(896), rs_buffers(384, (2,)), rs_buffers(768), rs_buffers(768),
        v((*cube, 512), BF16), v((*cube, 768), BF16), v((*cube, 768), BF16),
        v((2, 8, 3, 16, 384), BF16), v((2, 8, 3, 16, 128), BF16),
        v((2, Z, 2, 24, 768), F32), v((2, 4, 2, 24, 768), BF16), v((2, 4, 2, 24, 768), BF16),
        v((4, 2, 24, 768), BF16), v((4, 2, 24, 768), BF16), v((4, 2, 24, 768), BF16), v((4, 2, 24, 768), BF16),
        v((2, 24, 768), F32), v((24, 768), BF16), v((24, 768), BF16),
        v((NARROW, 24, 128), F32), v((NARROW, 24, 128), F32),
        v((2, 8, 128), F32), v((3, 8, 128), F32), v((Z - 1, 8, 128), F32),
        dma((6,)), dma((2, 10)), dma((2, 10)), dma((2, 5)), dma((2, 5)), dma((2, 5)), dma((2, 5)),
        dma((5, 3, 3)), dma((5, 3, 3)), dma((4, 3, 3)), dma((4, 3, 3)),
        dma((2, NARROW - 1)), dma((2, NARROW - 1)),
        dma((2, 2)), dma((2,)), dma((5,)), dma((5,)), dma((2,)), dma((3,)), dma((3,)),
        dma((Z - 1,)), dma((Z - 1,)),
    ]
    grad_shapes = [jax.ShapeDtypeStruct(g, BF16) for g in grads]
    outs = pl.pallas_call(
        functools.partial(kernel, full_width),
        out_shape=(*[v(g, BF16) for g in grads], v((8, 128), F32)),
        in_specs=[vm] * 5 + [pl.BlockSpec(memory_space=pltpu.HBM)] * 6,
        out_specs=[vm] * 8,
        scratch_shapes=scratch,
        compiler_params=pltpu.CompilerParams(
            collective_id=0, has_side_effects=True, vmem_limit_bytes=56 * 1024 * 1024
        ),
        name="layer",
    )(
        inputs, cotangent, norm_gain, q_gain.reshape(1, -1), k_gain.reshape(1, -1),
        w_query, w_key, w_value, w_out, w_up, w_down,
    )
    return pl.pallas_call(
        hand_over,
        out_shape=(
            *grad_shapes,
            jax.ShapeDtypeStruct((768,), F32), jax.ShapeDtypeStruct((128,), F32), jax.ShapeDtypeStruct((128,), F32),
        ),
        in_specs=[vm] * 8,
        out_specs=[anywhere] * 7 + [vm] * 3,
        scratch_shapes=[dma((7,))],
        name="hand_over",
    )(*[pltpu.with_memory_space_constraint(o, pltpu.VMEM) for o in outs])


def solution(mesh):
    return jax.shard_map(
        per_device,
        mesh=mesh,
        in_specs=(
            P("wide", "narrow"), P("wide", "narrow"), P("narrow"), P(), P(),
            P("narrow", "wide"), P("narrow", "wide"), P("narrow", "wide"), P("wide", "narrow"),
            P("narrow", "wide"), P("wide", "narrow"),
        ),
        out_specs=(
            P("wide", "narrow"),
            P("narrow", "wide"), P("narrow", "wide"), P("narrow", "wide"), P("wide", "narrow"),
            P("narrow", "wide"), P("wide", "narrow"),
            P("narrow"), P(), P(),
        ),
        check_vma=False,
    )
```

time: 125 us -> 103 us (0.82)
  local copies, waits for them, and re-layouts: 14.5 us -> 0 us
  Pallas kernels: 109 us -> 102 us
    unnamed x11 -> x0, local copies, waits for them, and re-layouts: 10.6 us -> none
    pallas_call x1 -> x2, Pallas kernels: 109 us -> 102 us  [the longest x1 99.7 us: per_device(): pl.pallas_call(functools.partial(kernel, full_width), out_shape=(*[v(g, B...]
    reshape x2 -> x0, local copies, waits for them, and re-layouts: 2.63 us -> none  [the longest x1 1.36 us: per_device(): return (*outs[:7], gains[:6].reshape(-1), gains[6], gains[7])]
    squeeze x1 -> x0, local copies, waits for them, and re-layouts: 1.26 us -> none  [per_device(): return (*outs[:7], gains[:6].reshape(-1), gains[6], gains[7])]
where the time goes in v2:
time: 103 us
  Pallas kernels  102 us (99%)
    pallas_call x1, Pallas kernels, per_device(): pl.pallas_call(functools.partial(kernel, full_width), out_shape=(*[v(g, B...  99.7 us
    pallas_call x1, Pallas kernels, per_device(): pl.pallas_call(hand_over, out_shape=(*grad_shapes, jax.ShapeDtypeStruct((...  2.32 us

profile of v2, /device:TPU:1, one launch (start us, length us, event | category | flops | bytes accessed | tf_op | source)
XLA Modules:
  0.0 102.7 jit_solution(18309242476005438410)
XLA Ops:
  0.6 99.7 %layer.1 = (bf16[24,768]{1,0:T(8,128)(2,1)S(1)}, bf16[768,128]{1,0:T(8,128)(2,1)S(1)}, bf16[768,128]{1,0:T(8,128)(2,1)S(1)}, bf16[768,128]{1,0:T(8,128)(2,1)S(1)...) custom-call(bf16[24,768]{1,0:T(8,128)(2,1)} %x_ref.1, ...), custom_call_target="tpu_custom_call" | custom-call | tf_op jit(solution)/shard_map/layer/pallas_call | solution.py:557
  100.3 2.3 %hand_over.1 = (bf16[24,768]{1,0:T(8,128)(2,1)}, bf16[768,128]{1,0:T(8,128)(2,1)}, bf16[768,128]{1,0:T(8,128)(2,1)}, bf16[768,128]{1,0:T(8,128)(2,1)}, bf16[128,...) custom-call(bf16[24,768]{1,0:T(8,128)(2,1)S(1)} %get-tuple-element.1, ...), custom_call_target="tpu_custom_call" | custom-call | tf_op jit(solution)/shard_map/hand_over/pallas_call | solution.py:571

commit v3 on v2

--- a/solution.py
+++ b/solution.py
@@ -55,13 +55,13 @@
     wf, wdn,
     cg, ng, cf, nf,
     pd, pq, pu,
-    bde, bdl, bq, bul, bue,
+    bde, bdl, bqe, bql, bul, bue,
     ga, gp, gh, dqkv, att,
     dp, sib_s, sib_r, x_s, x_r, z_s, z_r, fin, fin_s, fin_r,
-    st, st2, gtile, gquad, gz,
+    st, rows, tile, gquad, gz,
     wsem, sib_send, sib_recv, xp_send, xp_recv, line_send, line_recv,
     rs_send, rs_recv, ag_send, ag_recv, st_send, st_recv,
-    c_sem, x_sem, z_send, z_recv, f_sem, gq_send, gq_recv, gz_send, gz_recv,
+    c_send, c_recv, x_send, x_recv, z_send, z_recv, f_sem, gq_send, gq_recv, gz_send, gz_recv,
 ):
     w = lax.axis_index("wide")
     n = lax.axis_index("narrow")
@@ -190,39 +190,40 @@
     gather_own(ng, 1)
 
     every = slice(None)
+    even = ((0, 1, 2), (1, 2, 0), (2, 0, 1))
+    rs_orders = (even,) * 6
+    ag_orders = (even,) * 4
 
     def at(ref, half, part, fixed):
         return ref.at[(half,) + tuple(fixed.get(d, every) for d in range(3)) + (part,)]
-
-    def lead(half):
-        return (every,) if half is every else ()
 
     def rs_first(p, half, b, rnd):
         s1, r1 = b[0], b[1]
         for r in range(3):
-            s1[r] = at(p, half, r, {r: 1 - bits[r]})[...].astype(BF16)
-            send(s1.at[r], r1.at[r], rs_send.at[rnd, 0, r], rs_recv.at[rnd, 0, r], cube[r])
+            d = rs_orders[rnd][r][0]
+            s1[r] = at(p, half, r, {d: 1 - bits[d]})[...].astype(BF16)
+            send(s1.at[r], r1.at[r], rs_send.at[rnd, 0, r], rs_recv.at[rnd, 0, r], cube[d])
 
     def rs_second(p, half, b, rnd):
         r1, a1, s2, r2 = b[1:5]
         for r in range(3):
-            e = (r + 1) % 3
-            recv(r1.at[r], rs_send.at[rnd, 0, r], rs_recv.at[rnd, 0, r], cube[r])
-            rest = [d for d in range(3) if d != r]
-            pick = lambda v: (r,) + lead(half) + tuple(v if d == e else every for d in rest)
+            d, e, _ = rs_orders[rnd][r]
+            recv(r1.at[r], rs_send.at[rnd, 0, r], rs_recv.at[rnd, 0, r], cube[d])
+            rest = [i for i in range(3) if i != d]
+            pick = lambda v: (r,) + tuple(v if i == e else every for i in rest)
             away, stay = 1 - bits[e], bits[e]
             s2[r] = (
-                at(p, half, r, {r: bits[r], e: away})[...] + r1.at[pick(away)][...].astype(F32)
+                at(p, half, r, {d: bits[d], e: away})[...] + r1.at[pick(away)][...].astype(F32)
             ).astype(BF16)
             send(s2.at[r], r2.at[r], rs_send.at[rnd, 1, r], rs_recv.at[rnd, 1, r], cube[e])
-            a1[r] = at(p, half, r, {r: bits[r], e: stay})[...] + r1.at[pick(stay)][...].astype(F32)
+            a1[r] = at(p, half, r, {d: bits[d], e: stay})[...] + r1.at[pick(stay)][...].astype(F32)
 
     def rs_third(half, b, rnd):
         a1, r2, a2, s3, r3 = b[2], b[4], b[5], b[6], b[7]
         for r in range(3):
-            e, f = (r + 1) % 3, (r + 2) % 3
+            _, e, f = rs_orders[rnd][r]
             recv(r2.at[r], rs_send.at[rnd, 1, r], rs_recv.at[rnd, 1, r], cube[e])
-            away, stay = (r,) + lead(half) + (1 - bits[f],), (r,) + lead(half) + (bits[f],)
+            away, stay = (r, 1 - bits[f]), (r, bits[f])
             s3[r] = (a1[away] + r2[away].astype(F32)).astype(BF16)
             send(s3.at[r], r3.at[r], rs_send.at[rnd, 2, r], rs_recv.at[rnd, 2, r], cube[f])
             a2[r] = a1[stay] + r2[stay].astype(F32)
@@ -230,7 +231,7 @@
     def rs_last(b, rnd):
         a2, r3 = b[5], b[7]
         for r in range(3):
-            f = (r + 2) % 3
+            f = rs_orders[rnd][r][2]
             recv(r3.at[r], rs_send.at[rnd, 2, r], rs_recv.at[rnd, 2, r], cube[f])
             a2[r] = a2[r] + r3[r].astype(F32)
 
@@ -242,15 +243,25 @@
             lo = 128 + 256 * j
             pd[half, :, :, :, :, :, lo:lo + 256] = nt(lhs(), wdn[lo:lo + 256, :]).reshape(shape(256))
 
+    def query_products(half):
+        shape = lambda c: (2, 2, 2, 3, 16, c)
+        pq[half, :, :, :, :, :, 0:256] = nn(nf[half], wf[:, 0:256]).reshape(shape(256))
+        pq[half, :, :, :, :, :, 256:384] = nn(nf[half], wf[:, 256:384]).reshape(shape(128))
+
+    def up_products(half):
+        for j in range(3):
+            lo = 256 * j
+            pu[half, :, :, :, :, :, lo:lo + 256] = nn(nf[half], wf[:, 384 + lo:640 + lo]).reshape((2, 2, 2, 3, 16, 256))
+
     def ag(buf, half, rnd, step):
         for r in range(3):
-            order = ((r + 2) % 3, (r + 1) % 3, r)
+            order = ag_orders[rnd][r][::-1]
             src = at(buf, half, r, {d: bits[d] for d in order[step:]})
             send(src, src, ag_send.at[rnd, step, r], ag_recv.at[rnd, step, r], cube[order[step]])
 
     def ag_wait(buf, half, rnd, step):
         for r in range(3):
-            order = ((r + 2) % 3, (r + 1) % 3, r)
+            order = ag_orders[rnd][r][::-1]
             fixed = {d: bits[d] for d in order[step:]}
             fixed[order[step]] = 1 - bits[order[step]]
             recv(
@@ -268,17 +279,17 @@
         slope = 0.5 * (1.0 + t) + 0.5 * up * (1.0 - t * t) * (GELU_C * (1.0 + 3.0 * GELU_A * sq))
         gp[(half,) + mine] = (b_d[5][:, :, 128:896] * slope).astype(BF16)
 
+    gather_out(ng, 1)
     gather_line(cg, 0, 1)
     gather_line(cg, 0, 2)
-    gather_out(ng, 1)
+    gather_line(cg, 0, 3)
+    gather_line(cg, 0, 4)
     gather_x(cg, 0, 0)
-    gather_line(cg, 0, 3)
     gather_x(cg, 0, 1)
-    gather_line(cg, 0, 4)
     flatten_own(cg, 0, cf, 0)
     flatten_own(cg, 0, cf, 1)
+    flatten_own(cg, 0, cf, 2)
     gather_x(cg, 0, 2)
-    flatten_own(cg, 0, cf, 2)
     flatten_own(cg, 0, cf, 3)
     flatten_own(cg, 0, cf, 4)
     wcopies[0].wait()
@@ -286,75 +297,68 @@
     cot_products(xl)
     rs_first(pd, xl, bde, 0)
 
+    gather_line(ng, 1, 1)
     gather_x(cg, 0, 3)
-    gather_line(ng, 1, 1)
     gather_x(cg, 0, 4)
     gather_line(ng, 1, 2)
     gather_x(ng, 1, 0)
+    gather_line(ng, 1, 3)
+    gather_line(ng, 1, 4)
+    gather_x(ng, 1, 1)
     for k in range(FAR + 1):
         flatten_partner(cg, 0, cf, k)
-    gather_line(ng, 1, 3)
-    gather_x(ng, 1, 1)
-    gather_line(ng, 1, 4)
+    gather_x(ng, 1, 2)
     cot_products(theirs)
     rs_first(pd, theirs, bdl, 1)
 
-    gather_x(ng, 1, 2)
-    flatten_own(ng, 1, nf, 0)
-    flatten_own(ng, 1, nf, 1)
-    flatten_own(ng, 1, nf, 2)
     gather_x(ng, 1, 3)
-    flatten_own(ng, 1, nf, 3)
-    flatten_own(ng, 1, nf, 4)
     gather_x(ng, 1, 4)
+    for k in range(FAR + 1):
+        flatten_own(ng, 1, nf, k)
+    for c in wcopies[2:]:
+        c.wait()
+    query_products(xl)
+    rs_first(pq, xl, bqe, 2)
     rs_second(pd, xl, bde, 0)
+    up_products(xl)
+    rs_first(pu, xl, bue, 3)
     for k in range(FAR + 1):
         flatten_partner(ng, 1, nf, k)
-    for c in wcopies[2:]:
-        c.wait()
-    lhs = lambda: nf[...].reshape(768, 768)
-    shape = lambda c: (2, 2, 2, 2, 3, 16, c)
-    pq[:, :, :, :, :, :, 0:256] = nn(lhs(), wf[:, 0:256]).reshape(shape(256))
-    pq[:, :, :, :, :, :, 256:384] = nn(lhs(), wf[:, 256:384]).reshape(shape(128))
-    rs_first(pq, every, bq, 2)
+    query_products(theirs)
+    rs_first(pq, theirs, bql, 4)
     rs_second(pd, theirs, bdl, 1)
-    for j in range(3):
-        lo = 256 * j
-        pu[:, :, :, :, :, :, lo:lo + 256] = nn(lhs(), wf[:, 384 + lo:640 + lo]).reshape(shape(256))
-    rs_first(pu, theirs, bul, 3)
-    rs_first(pu, xl, bue, 4)
-
+    up_products(theirs)
+    rs_first(pu, theirs, bul, 5)
+
+    rs_second(pq, xl, bqe, 2)
     rs_third(xl, bde, 0)
-    rs_second(pq, every, bq, 2)
+    rs_second(pq, theirs, bql, 4)
+    rs_second(pu, xl, bue, 3)
     rs_third(theirs, bdl, 1)
-    rs_second(pu, theirs, bul, 3)
+    rs_third(xl, bqe, 2)
+    rs_second(pu, theirs, bul, 5)
+    rs_third(theirs, bql, 4)
+    rs_third(xl, bue, 3)
     rs_last(bde, 0)
-    rs_third(every, bq, 2)
     rs_last(bdl, 1)
-    rs_second(pu, xl, bue, 4)
-    rs_last(bq, 2)
-    for r in range(3):
-        ga[(every,) + mine + (r, every, pl.ds(0, 384))] = bq[5][r].astype(BF16)
-    ga[(xl,) + mine + (every, every, pl.ds(384, 128))] = bde[5][:, :, 0:128].astype(BF16)
-    ga[(theirs,) + mine + (every, every, pl.ds(384, 128))] = bdl[5][:, :, 0:128].astype(BF16)
+    rs_last(bqe, 2)
+    rs_third(theirs, bul, 5)
+    rs_last(bql, 4)
+    for half, b_q, b_d in ((xl, bqe, bde), (theirs, bql, bdl)):
+        ga[(half,) + mine + (every, every, pl.ds(0, 384))] = b_q[5][...].astype(BF16)
+        ga[(half,) + mine + (every, every, pl.ds(384, 128))] = b_d[5][:, :, 0:128].astype(BF16)
     ag(ga, every, 0, 0)
-    rs_third(theirs, bul, 3)
-    rs_third(xl, bue, 4)
-    ag_wait(ga, every, 0, 0)
-    ag(ga, every, 0, 1)
-    rs_last(bul, 3)
+    rs_last(bue, 3)
+    gelu(xl, bue, bde)
+    rs_last(bul, 5)
     gelu(theirs, bul, bdl)
     ag(gp, theirs, 1, 0)
-    rs_last(bue, 4)
-    gelu(xl, bue, bde)
     ag(gp, xl, 2, 0)
-    ag_wait(ga, every, 0, 1)
-    ag(ga, every, 0, 2)
-    ag_wait(gp, theirs, 1, 0)
-    ag(gp, theirs, 1, 1)
+    for step in range(2):
+        for buf, half, rnd in ((ga, every, 0), (gp, theirs, 1), (gp, xl, 2)):
+            ag_wait(buf, half, rnd, step)
+            ag(buf, half, rnd, step + 1)
     ag(gh, every, 3, 0)
-    ag_wait(gp, xl, 2, 0)
-    ag(gp, xl, 2, 1)
     ag_wait(ga, every, 0, 2)
 
     scale = HEAD ** (-0.5)
@@ -392,32 +396,38 @@
         store(dqkv, 0, norm_back(d_qnorm * qgain, q_unit, q_rstd).astype(BF16))
         store(dqkv, 128, norm_back(d_knorm * kgain, k_unit, k_rstd).astype(BF16))
 
-    attention(0)
-    ag_wait(gp, theirs, 1, 1)
-    ag(gp, theirs, 1, 2)
-    ag_wait(gh, every, 3, 0)
-    ag(gh, every, 3, 1)
-    attention(1)
-    ag_wait(gp, xl, 2, 1)
-    ag(gp, xl, 2, 2)
-    attention(2)
+    for image in range(3):
+        attention(image)
 
     gain_rows = []
+    ones = jnp.ones((8, 256), BF16)
+    tile_row = lax.broadcasted_iota(jnp.int32, (8, 384), 0)
+    tile_parts = []
 
     def products(half, e):
+        sum_gain = sum_normed = jnp.zeros((8, 384), F32)
         d_heads = lambda: dqkv[half].reshape(384, 384)
         d_up = lambda: gp[half].reshape(384, 768)
         for j in range(3):
             cols = slice(256 * j, 256 * j + 256)
             res = nt(d_heads(), wf[cols, 0:384]) + nt(d_up(), wf[cols, 384:1152])
             dp[e, :, :, :, cols] = res.reshape(Z, 2, 24, 256)
-            part = jnp.sum(res * nf[half, :, cols].astype(F32), axis=0, keepdims=True) / ngain[:, cols]
-            gain_rows.append(part)
-        for k in range(1, FAR):
-            sib_s[e, k - 1] = dp[e, zs(-way * k)].astype(BF16)
+            with_normed = res * nf[half, :, cols].astype(F32)
+            gain_rows.append(jnp.sum(with_normed, axis=0, keepdims=True) / ngain[:, cols])
+            sum_gain = sum_gain + nt(ones, (res * ngain[:, cols]).astype(BF16))
+            sum_normed = sum_normed + nt(ones, with_normed.astype(BF16))
+        tile_parts.append(
+            jnp.where(tile_row == 2 * half, sum_gain, jnp.where(tile_row == 2 * half + 1, sum_normed, 0.0))
+        )
         sib_s[e, FAR - 1, 0] = dp[e, zs(FAR), 1 - core].astype(BF16)
         sib_s[e, FAR - 1, 1] = dp[e, z, 1 - core].astype(BF16)
-        send(sib_s.at[e], sib_r.at[e], c_sem.at[e, 0], c_sem.at[e, 1], sibling)
+        for k in range(FAR, 0, -1):
+            if k < FAR:
+                sib_s[e, k - 1] = dp[e, zs(-way * k)].astype(BF16)
+            send(sib_s.at[e, k - 1], sib_r.at[e, k - 1], c_send.at[e, k - 1], c_recv.at[e, k - 1], sibling)
+
+    def from_sibling(e, k):
+        recv(sib_r.at[e, k - 1], c_send.at[e, k - 1], c_recv.at[e, k - 1], sibling)
 
     def pair(e, k):
         return dp[e, zs(way * k)] + sib_r[e, k - 1].astype(F32)
@@ -429,40 +439,41 @@
         return dp[e, z, core] + sib_r[e, FAR - 1, 1].astype(F32)
 
     ag_wait(gp, theirs, 1, 2)
+    ag_wait(gh, every, 3, 0)
+    ag(gh, every, 3, 1)
     products(theirs, 0)
+    for k in range(FAR, 0, -1):
+        from_sibling(0, k)
+        if k == FAR:
+            x_s[FAR - 1, 0] = far(0).astype(BF16)
+            x_s[FAR - 1, 1] = near(0).astype(BF16)
+        else:
+            x_s[k - 1] = pair(0, k).astype(BF16)
+        send(x_s.at[k - 1], x_r.at[k - 1], x_send.at[k - 1], x_recv.at[k - 1], xpartner)
+
+    ag_wait(gp, xl, 2, 2)
     ag_wait(gh, every, 3, 1)
-    recv(sib_r.at[0], c_sem.at[0, 0], c_sem.at[0, 1], sibling)
-    for k in range(1, FAR):
-        x_s[k - 1] = pair(0, k).astype(BF16)
-    x_s[FAR - 1, 0] = far(0).astype(BF16)
-    x_s[FAR - 1, 1] = near(0).astype(BF16)
-    send(x_s, x_r, x_sem.at[0], x_sem.at[1], xpartner)
-
-    ag_wait(gp, xl, 2, 2)
     ag(gh, every, 3, 2)
     products(xl, 1)
     gain_rows = [
         (gain_rows[j] + gain_rows[j + 3])[:, 128 * i:128 * i + 128] for j in range(3) for i in range(2)
     ]
-    gtile[0] = jnp.concatenate(gain_rows + gain_sums, axis=0)
-    for j in range(3):
-        send(gtile.at[0], gquad.at[j], gq_send.at[j], gq_recv.at[j], quad[j])
-    recv(x_r, x_sem.at[0], x_sem.at[1], xpartner)
-    recv(sib_r.at[1], c_sem.at[1, 0], c_sem.at[1, 1], sibling)
-    for k in range(FAR - 1, 0, -1):
-        z_s[k - 1] = (pair(1, k) + x_r[k - 1].astype(F32)).astype(BF16)
-        send(z_s.at[k - 1], z_r.at[k - 1], z_send.at[k], z_recv.at[k], (dev(zs(way * k), xl, core), n))
-    z_s[FAR - 1, 0] = (far(1) + x_r[FAR - 1, 0].astype(F32)).astype(BF16)
-    send(
-        z_s.at[FAR - 1, 0], z_r.at[FAR - 1, 0], z_send.at[FAR], z_recv.at[FAR], (dev(zs(FAR), xl, core), n)
-    )
+    gain_tile = jnp.concatenate(gain_rows + gain_sums, axis=0)
+    gain_tile = jnp.concatenate([gain_tile[0:4], gain_tile[4:8], jnp.zeros((4, 128), F32)], axis=1)
+    tile[0] = tile_parts[0] + tile_parts[1] + jnp.concatenate([jnp.zeros((4, 384), F32), gain_tile], axis=0)
+    for k in range(1, Z):
+        send(tile.at[0], gz.at[k - 1], gz_send.at[k - 1], gz_recv.at[k - 1], z_peers[k - 1])
+    for k in range(FAR, 0, -1):
+        recv(x_r.at[k - 1], x_send.at[k - 1], x_recv.at[k - 1], xpartner)
+        from_sibling(1, k)
+        if k == FAR:
+            z_s[FAR - 1, 0] = (far(1) + x_r[FAR - 1, 0].astype(F32)).astype(BF16)
+            src, dst = z_s.at[FAR - 1, 0], z_r.at[FAR - 1, 0]
+        else:
+            z_s[k - 1] = (pair(1, k) + x_r[k - 1].astype(F32)).astype(BF16)
+            src, dst = z_s.at[k - 1], z_r.at[k - 1]
+        send(src, dst, z_send.at[k], z_recv.at[k], (dev(zs(way * k), xl, core), n))
     fin[core] = near(1) + x_r[FAR - 1, 1].astype(F32)
-    for j in range(3):
-        recv(gquad.at[j], gq_send.at[j], gq_recv.at[j], quad[j])
-    gtile[1] = gtile[0] + gquad[0] + gquad[1] + gquad[2]
-    for k in range(1, Z):
-        send(gtile.at[1], gz.at[k - 1], gz_send.at[k - 1], gz_recv.at[k - 1], z_peers[k - 1])
-
     for j in range(3):
         cols = slice(256 * j, 256 * j + 256)
         left = nf[:, :, cols].reshape(768, 256)
@@ -471,6 +482,25 @@
         gq[cols, :] = res[:, 0:128]
         gk[cols, :] = res[:, 128:256]
         gv[cols, :] = res[:, 256:384]
+    for k in range(1, Z):
+        recv(gz.at[k - 1], gz_send.at[k - 1], gz_recv.at[k - 1], z_peers[Z - 1 - k])
+    tile[1] = tile[0] + jnp.sum(gz[...], axis=0)
+    for j in range(3):
+        send(tile.at[1], gquad.at[j], gq_send.at[j], gq_recv.at[j], quad[j])
+    ag_wait(gh, every, 3, 2)
+    for j in range(3):
+        cols = slice(256 * j, 256 * j + 256)
+        hidden = gh[:, :, :, :, :, :, cols].reshape(768, 256)
+        gd[cols, :] = tn(hidden, cf[...].reshape(768, 768)).astype(BF16)
+    for j in range(3):
+        recv(gquad.at[j], gq_send.at[j], gq_recv.at[j], quad[j])
+    wide_total = tile[1] + gquad[0] + gquad[1] + gquad[2]
+    rows[0] = wide_total
+    gains[0:4] = wide_total[4:8, 0:128]
+    gains[4:8] = wide_total[4:8, 128:256]
+    for k, p in enumerate(n_peers):
+        send(rows.at[0], rows.at[k + 1], st_send.at[1, k], st_recv.at[1, k], p)
+    go[...] = tn(att[...].reshape(768, 128), cf[...].reshape(768, 768)).astype(BF16)
 
     recv(z_r.at[FAR - 1, 0], z_send.at[FAR], z_recv.at[FAR], (dev(zs(FAR), xl, core), n))
     for k in range(1, FAR):
@@ -479,27 +509,19 @@
     fin_s[...] = fin[1 - core].astype(BF16)
     send(fin_s, fin_r, f_sem.at[0], f_sem.at[1], sibling)
 
-    go[...] = tn(att[...].reshape(768, 128), cf[...].reshape(768, 768)).astype(BF16)
-
     d_own = fin[core] + z_r[FAR - 1, 0].astype(F32) + sum(z_r[k, core].astype(F32) for k in range(FAR - 1))
     recv(fin_r, f_sem.at[0], f_sem.at[1], sibling)
     d_normed = d_own + fin_r[...].astype(F32)
     d_unit = d_normed * ngain
     unit = (x_ref[...].astype(F32) - row_mean) * row_rstd
-    small_sum(st2, 1, jnp.sum(d_unit, axis=1, keepdims=True), jnp.sum(d_unit * unit, axis=1, keepdims=True))
-
-    ag_wait(gh, every, 3, 2)
-    for j in range(3):
-        cols = slice(256 * j, 256 * j + 256)
-        hidden = gh[:, :, :, :, :, :, cols].reshape(768, 256)
-        gd[cols, :] = tn(hidden, cf[...].reshape(768, 768)).astype(BF16)
-    total = gtile[1]
-    for k in range(1, Z):
-        recv(gz.at[k - 1], gz_send.at[k - 1], gz_recv.at[k - 1], z_peers[Z - 1 - k])
-        total = total + gz[k - 1]
-    gains[...] = total
-
-    first, second = small_total(st2, 1)
+
+    for k in range(NARROW - 1):
+        recv(rows.at[k + 1], st_send.at[1, k], st_recv.at[1, k], (w, (n - 1 - k + NARROW) % NARROW))
+    tile[2] = jnp.sum(rows[...], axis=0)
+    own_row = lax.broadcasted_iota(jnp.int32, (24, 384), 0) + (48 * z + 24 * core)
+    own_row = own_row == lax.broadcasted_iota(jnp.int32, (24, 384), 1)
+    pick_row = lambda i: jnp.sum(jnp.where(own_row, tile[2, pl.ds(2 * xl + i, 1), :], 0.0), axis=1, keepdims=True) / full_width
+    first, second = pick_row(0), pick_row(1)
     dx[...] = (cot_ref[...].astype(F32) + row_rstd * (d_unit - first - unit * second)).astype(BF16)
 
     for c in pending:
@@ -526,11 +548,11 @@
     v = pltpu.VMEM
     dma = pltpu.SemaphoreType.DMA
 
-    def rs_buffers(c, lead=()):
+    def rs_buffers(c):
         return [
-            v((3, *lead, 2, 2, 16, c), BF16), v((3, *lead, 2, 2, 16, c), BF16), v((3, *lead, 2, 16, c), F32),
-            v((3, *lead, 2, 16, c), BF16), v((3, *lead, 2, 16, c), BF16), v((3, *lead, 16, c), F32),
-            v((3, *lead, 16, c), BF16), v((3, *lead, 16, c), BF16),
+            v((3, 2, 2, 16, c), BF16), v((3, 2, 2, 16, c), BF16), v((3, 2, 16, c), F32),
+            v((3, 2, 16, c), BF16), v((3, 2, 16, c), BF16), v((3, 16, c), F32),
+            v((3, 16, c), BF16), v((3, 16, c), BF16),
         ]
 
     grads = [(24, 768), (768, 128), (768, 128), (768, 128), (128, 768), (768, 768), (768, 768)]
@@ -539,18 +561,18 @@
         v((768, 1152), BF16), v((896, 768), BF16),
         v((Z, 2, 2, 24, 768), BF16), v((Z, 2, 2, 24, 768), BF16), v((2, 384, 768), BF16), v((2, 384, 768), BF16),
         v((*cube, 896), F32), v((*cube, 384), F32), v((*cube, 768), F32),
-        rs_buffers(896), rs_buffers(896), rs_buffers(384, (2,)), rs_buffers(768), rs_buffers(768),
+        rs_buffers(896), rs_buffers(896), rs_buffers(384), rs_buffers(384), rs_buffers(768), rs_buffers(768),
         v((*cube, 512), BF16), v((*cube, 768), BF16), v((*cube, 768), BF16),
         v((2, 8, 3, 16, 384), BF16), v((2, 8, 3, 16, 128), BF16),
         v((2, Z, 2, 24, 768), F32), v((2, 4, 2, 24, 768), BF16), v((2, 4, 2, 24, 768), BF16),
         v((4, 2, 24, 768), BF16), v((4, 2, 24, 768), BF16), v((4, 2, 24, 768), BF16), v((4, 2, 24, 768), BF16),
         v((2, 24, 768), F32), v((24, 768), BF16), v((24, 768), BF16),
-        v((NARROW, 24, 128), F32), v((NARROW, 24, 128), F32),
-        v((2, 8, 128), F32), v((3, 8, 128), F32), v((Z - 1, 8, 128), F32),
+        v((NARROW, 24, 128), F32), v((NARROW, 8, 384), F32),
+        v((3, 8, 384), F32), v((3, 8, 384), F32), v((Z - 1, 8, 384), F32),
         dma((6,)), dma((2, 10)), dma((2, 10)), dma((2, 5)), dma((2, 5)), dma((2, 5)), dma((2, 5)),
-        dma((5, 3, 3)), dma((5, 3, 3)), dma((4, 3, 3)), dma((4, 3, 3)),
+        dma((6, 3, 3)), dma((6, 3, 3)), dma((4, 3, 3)), dma((4, 3, 3)),
         dma((2, NARROW - 1)), dma((2, NARROW - 1)),
-        dma((2, 2)), dma((2,)), dma((5,)), dma((5,)), dma((2,)), dma((3,)), dma((3,)),
+        dma((2, 4)), dma((2, 4)), dma((4,)), dma((4,)), dma((5,)), dma((5,)), dma((2,)), dma((3,)), dma((3,)),
         dma((Z - 1,)), dma((Z - 1,)),
     ]
     grad_shapes = [jax.ShapeDtypeStruct(g, BF16) for g in grads]

time: 103 us -> 99.6 us (0.967)
  Pallas kernels: 102 us -> 98.8 us
    pallas_call x1, Pallas kernels: 99.7 us -> 96.5 us  [per_device(): pl.pallas_call(functools.partial(kernel, full_width), out_shape=(*[v(g, B...]
where the time goes in v3:
time: 99.6 us; the launch traced here: 99.5 us
  Pallas kernels  98.8 us (99%)
    pallas_call x1, Pallas kernels, per_device(): pl.pallas_call(functools.partial(kernel, full_width), out_shape=(*[v(g, B...  96.5 us
    pallas_call x1, Pallas kernels, per_device(): pl.pallas_call(hand_over, out_shape=(*grad_shapes, jax.ShapeDtypeStruct((...  2.32 us

profile of v3, /device:TPU:1, one launch (start us, length us, event | category | flops | bytes accessed | tf_op | source)
XLA Modules:
  0.0 99.5 jit_solution(4569920411462922194)
XLA Ops:
  0.6 96.5 %layer.1 = (bf16[24,768]{1,0:T(8,128)(2,1)S(1)}, bf16[768,128]{1,0:T(8,128)(2,1)S(1)}, bf16[768,128]{1,0:T(8,128)(2,1)S(1)}, bf16[768,128]{1,0:T(8,128)(2,1)S(1)...) custom-call(bf16[24,768]{1,0:T(8,128)(2,1)} %x_ref.1, ...), custom_call_target="tpu_custom_call" | custom-call | tf_op jit(solution)/shard_map/layer/pallas_call | solution.py:579
  97.2 2.3 %hand_over.1 = (bf16[24,768]{1,0:T(8,128)(2,1)}, bf16[768,128]{1,0:T(8,128)(2,1)}, bf16[768,128]{1,0:T(8,128)(2,1)}, bf16[768,128]{1,0:T(8,128)(2,1)}, bf16[128,...) custom-call(bf16[24,768]{1,0:T(8,128)(2,1)S(1)} %get-tuple-element.1, ...), custom_call_target="tpu_custom_call" | custom-call | tf_op jit(solution)/shard_map/hand_over/pallas_call | solution.py:593

commit v4 on v3

--- a/solution.py
+++ b/solution.py
@@ -354,11 +354,13 @@
     gelu(theirs, bul, bdl)
     ag(gp, theirs, 1, 0)
     ag(gp, xl, 2, 0)
+    ag(gh, every, 3, 0)
     for step in range(2):
         for buf, half, rnd in ((ga, every, 0), (gp, theirs, 1), (gp, xl, 2)):
             ag_wait(buf, half, rnd, step)
             ag(buf, half, rnd, step + 1)
-    ag(gh, every, 3, 0)
+    ag_wait(gh, every, 3, 0)
+    ag(gh, every, 3, 1)
     ag_wait(ga, every, 0, 2)
 
     scale = HEAD ** (-0.5)
@@ -439,8 +441,6 @@
         return dp[e, z, core] + sib_r[e, FAR - 1, 1].astype(F32)
 
     ag_wait(gp, theirs, 1, 2)
-    ag_wait(gh, every, 3, 0)
-    ag(gh, every, 3, 1)
     products(theirs, 0)
     for k in range(FAR, 0, -1):
         from_sibling(0, k)
@@ -451,9 +451,9 @@
             x_s[k - 1] = pair(0, k).astype(BF16)
         send(x_s.at[k - 1], x_r.at[k - 1], x_send.at[k - 1], x_recv.at[k - 1], xpartner)
 
-    ag_wait(gp, xl, 2, 2)
     ag_wait(gh, every, 3, 1)
     ag(gh, every, 3, 2)
+    ag_wait(gp, xl, 2, 2)
     products(xl, 1)
     gain_rows = [
         (gain_rows[j] + gain_rows[j + 3])[:, 128 * i:128 * i + 128] for j in range(3) for i in range(2)
@@ -487,11 +487,6 @@
     tile[1] = tile[0] + jnp.sum(gz[...], axis=0)
     for j in range(3):
         send(tile.at[1], gquad.at[j], gq_send.at[j], gq_recv.at[j], quad[j])
-    ag_wait(gh, every, 3, 2)
-    for j in range(3):
-        cols = slice(256 * j, 256 * j + 256)
-        hidden = gh[:, :, :, :, :, :, cols].reshape(768, 256)
-        gd[cols, :] = tn(hidden, cf[...].reshape(768, 768)).astype(BF16)
     for j in range(3):
         recv(gquad.at[j], gq_send.at[j], gq_recv.at[j], quad[j])
     wide_total = tile[1] + gquad[0] + gquad[1] + gquad[2]
@@ -510,6 +505,11 @@
     send(fin_s, fin_r, f_sem.at[0], f_sem.at[1], sibling)
 
     d_own = fin[core] + z_r[FAR - 1, 0].astype(F32) + sum(z_r[k, core].astype(F32) for k in range(FAR - 1))
+    ag_wait(gh, every, 3, 2)
+    for j in range(3):
+        cols = slice(256 * j, 256 * j + 256)
+        hidden = gh[:, :, :, :, :, :, cols].reshape(768, 256)
+        gd[cols, :] = tn(hidden, cf[...].reshape(768, 768)).astype(BF16)
     recv(fin_r, f_sem.at[0], f_sem.at[1], sibling)
     d_normed = d_own + fin_r[...].astype(F32)
     d_unit = d_normed * ngain

time: 99.6 us -> 96.7 us (0.971)
  Pallas kernels: 98.8 us -> 95.9 us
    pallas_call x1, Pallas kernels: 96.5 us -> 93.6 us  [per_device(): pl.pallas_call(functools.partial(kernel, full_width), out_shape=(*[v(g, B...]
where the time goes in v4:
time: 96.7 us; the launch traced here: 96.5 us
  Pallas kernels  95.9 us (99%)
    pallas_call x1, Pallas kernels, per_device(): pl.pallas_call(functools.partial(kernel, full_width), out_shape=(*[v(g, B...  93.6 us
    pallas_call x1, Pallas kernels, per_device(): pl.pallas_call(hand_over, out_shape=(*grad_shapes, jax.ShapeDtypeStruct((...  2.32 us

profile of v4, /device:TPU:1, one launch (start us, length us, event | category | flops | bytes accessed | tf_op | source)
XLA Modules:
  0.0 96.5 jit_solution(1065540564039524020)
XLA Ops:
  0.6 93.6 %layer.1 = (bf16[24,768]{1,0:T(8,128)(2,1)S(1)}, bf16[768,128]{1,0:T(8,128)(2,1)S(1)}, bf16[768,128]{1,0:T(8,128)(2,1)S(1)}, bf16[768,128]{1,0:T(8,128)(2,1)S(1)...) custom-call(bf16[24,768]{1,0:T(8,128)(2,1)} %x_ref.1, ...), custom_call_target="tpu_custom_call" | custom-call | tf_op jit(solution)/shard_map/layer/pallas_call | solution.py:579
  94.2 2.3 %hand_over.1 = (bf16[24,768]{1,0:T(8,128)(2,1)}, bf16[768,128]{1,0:T(8,128)(2,1)}, bf16[768,128]{1,0:T(8,128)(2,1)}, bf16[768,128]{1,0:T(8,128)(2,1)}, bf16[128,...) custom-call(bf16[24,768]{1,0:T(8,128)(2,1)S(1)} %get-tuple-element.1, ...), custom_call_target="tpu_custom_call" | custom-call | tf_op jit(solution)/shard_map/hand_over/pallas_call | solution.py:593
